TPU v7x, 32 devices: a whole 2x2x4 slice. The times are simulated.
32 devices in a mesh: rep: 2 (over x), dp: 4 (over y, core), ctx: 4 (over z).
Axes of the slice: x: 2, y: 2, z: 4, core: 2. Of those that a mesh axis runs over, the one named last changes fastest.
Arguments:
- frames: bfloat16 [8, 512, 1024], P(('rep', 'dp'), 'ctx'), may hold values from -24 to 24
- lengths: int32 [8], P(('rep', 'dp')), may hold values from 64 to 512, as said below
- cotangent: bfloat16 [8, 512, 1024], P(('rep', 'dp'), 'ctx'), may hold values from -6 to 6
- w_query: bfloat16 [1024, 512], P('dp'), may hold values from -0.5 to 0.5
- w_key: bfloat16 [1024, 512], P('dp'), may hold values from -0.5 to 0.5
- w_value: bfloat16 [1024, 512], P('dp'), may hold values from -0.1875 to 0.1875
- w_out: bfloat16 [512, 1024], P('dp'), may hold values from -0.25 to 0.25
Outputs:
- attended: bfloat16 [8, 512, 1024], P(('rep', 'dp'), 'ctx')
- grad_frames: bfloat16 [8, 512, 1024], P(('rep', 'dp'), 'ctx')
- grad_out: float32 [512, 1024], P('dp')
Inputs may be any that keep to these rules, and one draw needn't show every extreme that they name: `lengths`: number of real frames of each meeting; one meeting of every draw has all 512 frames real.
All inputs are finite; a program needn't handle non-finite values.
Results may differ from a plain program's by a relative error of at most 0.025.
The roundings to bfloat16 on the way count: a program that leaves them out, or rounds other values in their place, can miss the bound.
Values may be sent and summed in bfloat16 or wider, within the bound.
A program may use at most 64 MiB of HBM per device.

v0:
```python
import functools
import math

import jax
import jax.numpy as jnp
from jax import lax
from jax.experimental import pallas as pl
from jax.experimental.pallas import tpu as pltpu
from jax.sharding import PartitionSpec as P

HEAD = 128


MASKED_SCORE = -1e30


def head_split(matrix, head_count):
    return matrix.reshape(matrix.shape[0], head_count, matrix.shape[1] // head_count)


def forward_step(carry, key_part, value_part, offset, query_heads, length, score_scale):
    head_count = query_heads.shape[1]
    amount = key_part.shape[0]
    maxima, totals, accumulated = carry
    key_heads = head_split(key_part, head_count)
    value_heads = head_split(value_part, head_count)
    scores = (
        jnp.einsum("rhe,nhe->hrn", query_heads, key_heads, preferred_element_type=jnp.float32)
        * score_scale
    )
    usable = offset + jnp.arange(amount) < length
    scores = jnp.where(usable[None, None, :], scores, MASKED_SCORE)
    new_maxima = jnp.maximum(maxima, jnp.max(scores, axis=2))
    factor = jnp.exp(maxima - new_maxima)
    exponent = jnp.where(usable[None, None, :], jnp.exp(scores - new_maxima[:, :, None]), 0.0)
    totals = totals * factor + jnp.sum(exponent, axis=2)
    mixed = jnp.einsum(
        "hrn,nhe->hre",
        exponent.astype(jnp.bfloat16),
        value_heads,
        preferred_element_type=jnp.float32,
    )
    accumulated = accumulated * factor[:, :, None] + mixed
    return (new_maxima, totals, accumulated)


def query_step(
    grad_accum,
    key_part,
    value_part,
    offset,
    query_heads,
    context_heads,
    logsum,
    deltas,
    length,
    score_scale,
):
    head_count = query_heads.shape[1]
    amount = key_part.shape[0]
    key_heads = head_split(key_part, head_count)
    value_heads = head_split(value_part, head_count)
    scores = (
        jnp.einsum("rhe,nhe->hrn", query_heads, key_heads, preferred_element_type=jnp.float32)
        * score_scale
    )
    usable = offset + jnp.arange(amount) < length
    attention = jnp.where(usable[None, None, :], jnp.exp(scores - logsum[:, :, None]), 0.0)
    grad_prob = jnp.einsum(
        "rhe,nhe->hrn", context_heads, value_heads, preferred_element_type=jnp.float32
    )
    grad_score = (attention * (grad_prob - deltas[:, :, None])).astype(jnp.bfloat16)
    added = jnp.einsum("hrn,nhe->rhe", grad_score, key_heads, preferred_element_type=jnp.float32)
    return grad_accum + added * score_scale


def key_step(
    query_part,
    context_part,
    all_logsum,
    all_deltas,
    key_heads,
    value_heads,
    key_usable,
    score_scale,
):
    head_count = key_heads.shape[1]
    query_heads = head_split(query_part, head_count)
    context_heads = head_split(context_part, head_count)
    scores = (
        jnp.einsum("rhe,nhe->hrn", query_heads, key_heads, preferred_element_type=jnp.float32)
        * score_scale
    )
    attention = jnp.where(key_usable[None, None, :], jnp.exp(scores - all_logsum[:, :, None]), 0.0)
    grad_value = jnp.einsum(
        "hrn,rhe->nhe",
        attention.astype(jnp.bfloat16),
        context_heads,
        preferred_element_type=jnp.float32,
    )
    grad_prob = jnp.einsum(
        "rhe,nhe->hrn", context_heads, value_heads, preferred_element_type=jnp.float32
    )
    grad_score = (attention * (grad_prob - all_deltas[:, :, None])).astype(jnp.bfloat16)
    added = jnp.einsum("hrn,rhe->nhe", grad_score, query_heads, preferred_element_type=jnp.float32)
    return (added * score_scale, grad_value)


def back_project(gradient, weight):
    return lax.dot_general(
        gradient, weight, (((1,), (1,)), ((), ())), preferred_element_type=jnp.float32
    )


def shards(frames, lengths, cotangent, w_query, w_key, w_value, w_out):
    full_query, full_key, full_value, full_out = (
        lax.all_gather(w_query, "dp", axis=0, tiled=True),
        lax.all_gather(w_key, "dp", axis=0, tiled=True),
        lax.all_gather(w_value, "dp", axis=0, tiled=True),
        lax.all_gather(w_out, "dp", axis=0, tiled=True),
    )
    inputs = frames[0]
    upstream = cotangent[0]
    length = lengths[0]
    row_count = inputs.shape[0]
    inner_width = full_query.shape[1]
    head_count = inner_width // HEAD
    score_scale = HEAD ** (-0.5)
    first_frame = lax.axis_index("ctx") * row_count
    row_usable = first_frame + jnp.arange(row_count) < length
    queries = jnp.dot(inputs, full_query, preferred_element_type=jnp.float32).astype(jnp.bfloat16)
    keys = jnp.dot(inputs, full_key, preferred_element_type=jnp.float32).astype(jnp.bfloat16)
    values = jnp.dot(inputs, full_value, preferred_element_type=jnp.float32).astype(jnp.bfloat16)
    query_heads = head_split(queries, head_count)
    key_heads = head_split(keys, head_count)
    value_heads = head_split(values, head_count)
    start_state = (
        jnp.full((head_count, row_count), MASKED_SCORE, jnp.float32),
        jnp.zeros((head_count, row_count), jnp.float32),
        jnp.zeros((head_count, row_count, HEAD), jnp.float32),
    )
    all_keys, all_values = (
        lax.all_gather(keys, "ctx", axis=0, tiled=True),
        lax.all_gather(values, "ctx", axis=0, tiled=True),
    )
    key_block = row_count * math.gcd(max(1, 512 // row_count), lax.axis_size("ctx"))
    block_count = all_keys.shape[0] // key_block
    key_blocks = all_keys.reshape(block_count, key_block, inner_width)
    value_blocks = all_values.reshape(block_count, key_block, inner_width)
    block_starts = jnp.arange(block_count, dtype=jnp.int32) * key_block

    def scan_forward(current, scan_item):
        return (
            forward_step(
                current, scan_item[0], scan_item[1], scan_item[2], query_heads, length, score_scale
            ),
            None,
        )

    softmax_state, unused = lax.scan(
        scan_forward, start_state, (key_blocks, value_blocks, block_starts)
    )
    maxima, totals, accumulated = softmax_state
    context = (
        (accumulated / totals[:, :, None])
        .transpose(1, 0, 2)
        .reshape(row_count, inner_width)
        .astype(jnp.bfloat16)
    )
    logsum = maxima + jnp.log(totals)
    attended = jnp.dot(context, full_out, preferred_element_type=jnp.float32)
    attended = jnp.where(row_usable[:, None], attended, 0.0).astype(jnp.bfloat16)
    masked_grad = jnp.where(row_usable[:, None], upstream, jnp.zeros_like(upstream))
    grad_context = back_project(masked_grad, full_out).astype(jnp.bfloat16)
    deltas = jnp.sum(
        (grad_context.astype(jnp.float32) * context.astype(jnp.float32)).reshape(
            row_count, head_count, HEAD
        ),
        axis=2,
    )
    context_heads = head_split(grad_context, head_count)
    delta_heads = deltas.T
    all_logsum, all_deltas = (
        lax.all_gather(logsum, "ctx", axis=1, tiled=True),
        lax.all_gather(delta_heads, "ctx", axis=1, tiled=True),
    )
    zero_grad = jnp.zeros((row_count, head_count, HEAD), jnp.float32)

    def scan_query(current, scan_item):
        return (
            query_step(
                current,
                scan_item[0],
                scan_item[1],
                scan_item[2],
                query_heads,
                context_heads,
                logsum,
                delta_heads,
                length,
                score_scale,
            ),
            None,
        )

    grad_query, unused = lax.scan(scan_query, zero_grad, (key_blocks, value_blocks, block_starts))
    grad_key, grad_value = key_step(
        lax.all_gather(queries, "ctx", axis=0, tiled=True),
        lax.all_gather(grad_context, "ctx", axis=0, tiled=True),
        all_logsum,
        all_deltas,
        key_heads,
        value_heads,
        row_usable,
        score_scale,
    )
    grad_query = grad_query.reshape(row_count, inner_width).astype(jnp.bfloat16)
    grad_key = grad_key.reshape(row_count, inner_width).astype(jnp.bfloat16)
    grad_value = grad_value.reshape(row_count, inner_width).astype(jnp.bfloat16)
    grad_input = (
        back_project(grad_query, full_query)
        + back_project(grad_key, full_key)
        + back_project(grad_value, full_value)
    )
    grad_frames = grad_input.astype(jnp.bfloat16)
    summed_grad = lax.psum(
        lax.dot_general(
            context, masked_grad, (((0,), (0,)), ((), ())), preferred_element_type=jnp.float32
        ),
        ("rep", "ctx"),
    )
    grad_out = lax.psum_scatter(summed_grad, "dp", scatter_dimension=0, tiled=True)
    return (attended[None], grad_frames[None], grad_out)


MESH = pl.DeviceIdType.MESH


def dot(left, right, left_dim, right_dim):
    return lax.dot_general(
        left, right, (((left_dim,), (right_dim,)), ((), ())), preferred_element_type=jnp.float32
    )


def fused_kernel(
    frames_ref,
    length_ref,
    cot_ref,
    wq_ref,
    wk_ref,
    wv_ref,
    wo_ref,
    attended_ref,
    grad_frames_ref,
    grad_out_ref,
    xs,
    upstream,
    mine,
    cs,
    wq,
    wk,
    wv,
    wo,
    qs,
    ks,
    vs,
    gs,
    ctx,
    logsum,
    deltas,
    dq,
    dk,
    dv,
    part,
    part_in,
    slices,
    send_sem,
    recv_sem,
    local_sem,
):
    rep, dp, z = lax.axis_index("rep"), lax.axis_index("dp"), lax.axis_index("ctx")
    count = 4
    heads = 4
    rows = frames_ref.shape[1]
    full = rows * count
    width = slices.shape[2]
    scale = HEAD ** (-0.5)
    sibling = dp + 1 - 2 * lax.rem(dp, 2)
    across = lax.rem(dp + 2, 4)
    across_sibling = lax.rem(sibling + 2, 4)
    other_rep = 1 - rep
    group = rep * 4 + dp

    local = [
        pltpu.make_async_copy(source, target, local_sem.at[at])
        for at, (source, target) in enumerate(
            (
                (wk_ref, wk.at[dp]),
                (wv_ref, wv.at[dp]),
                (wq_ref, wq.at[dp]),
                (wo_ref, wo.at[dp]),
                (frames_ref.at[0], xs.at[z]),
                (cot_ref.at[0], upstream),
            )
        )
    ]
    for copy in local:
        copy.start()

    barrier = pltpu.get_barrier_semaphore()
    for step in range(1, count):
        pl.semaphore_signal(
            barrier, inc=1, device_id=(rep, dp, lax.rem(z + step, count)), device_id_type=MESH
        )
    for step in range(1, 8):
        peer = lax.rem(group + step, 8)
        pl.semaphore_signal(
            barrier, inc=1, device_id=(peer // 4, lax.rem(peer, 4), z), device_id_type=MESH
        )
    pl.semaphore_wait(barrier, 10)

    def remote(source, target, index, device):
        return pltpu.make_async_remote_copy(
            src_ref=source,
            dst_ref=target,
            send_sem=send_sem.at[index],
            recv_sem=recv_sem.at[index],
            device_id=device,
            device_id_type=MESH,
        )

    def chain(which, side, hop):
        sign = 1 - 2 * side
        pool = (xs, gs)[which]
        owner = z - sign * (hop - 1)
        slot = jnp.clip(owner, 0, count - 1)
        source = frames_ref.at[0] if which == 0 and hop == 1 else pool.at[slot]
        target = jnp.clip(z + sign, 0, count - 1)
        index = which * 6 + side * 3 + hop - 1
        valid = (z + sign >= 0) & (z + sign < count) & (owner >= 0) & (owner < count)
        return valid, remote(source, pool.at[slot], index, (rep, dp, target))

    def chain_send(which, hop):
        for side in range(2):
            valid, copy = chain(which, side, hop)

            @pl.when(valid)
            def _():
                copy.start()

    def chain_recv(which, hop):
        for side in range(2):
            sign = 1 - 2 * side
            pool = (xs, gs)[which]
            owner = z - sign * hop
            slot = jnp.clip(owner, 0, count - 1)
            index = which * 6 + side * 3 + hop - 1

            @pl.when((owner >= 0) & (owner < count))
            def _():
                remote(pool.at[slot], pool.at[slot], index, (rep, dp, z)).wait_recv()

    weights = ((wo_ref, wo), (wk_ref, wk), (wv_ref, wv), (wq_ref, wq))

    def half(ref, which):
        size = ref.shape[0] // 2
        return ref.at[pl.ds(pl.multiple_of(which * size, size), size)]

    def chunk(ref, which, at):
        size = ref.shape[0] // 4
        return ref.at[pl.ds(pl.multiple_of((which * 2 + at) * size, size), size)]

    def weight_copy(piece, step):
        shard, pool = weights[piece]
        index = 12 + piece * 7 + step
        if step == 0:
            return remote(shard, pool.at[dp], index, (rep, sibling, z))
        if step < 3:
            target = chunk(pool.at[dp], rep, step - 1)
            return remote(chunk(shard, rep, step - 1), target, index, (rep, across, z))
        mine_at = pool.at[across]
        if step < 5:
            source = chunk(mine_at, rep, step - 3)
            return remote(source, source, index, (other_rep, dp, z))
        source = half(mine_at, rep if step == 5 else other_rep)
        return remote(source, source, index, (rep, sibling, z))

    def weight_recv(piece, step):
        pool = weights[piece][1]
        index = 12 + piece * 7 + step
        if step == 0:
            target = pool.at[sibling]
        elif step < 3:
            target = chunk(pool.at[across], rep, step - 1)
        elif step < 5:
            target = chunk(pool.at[across], other_rep, step - 3)
        else:
            target = half(pool.at[across_sibling], rep if step == 5 else other_rep)
        remote(target, target, index, (rep, dp, z)).wait_recv()

    def finish_chunk(at):
        weight_recv(at // 2, 3 + at % 2)
        if at % 2 == 1:
            weight_copy(at // 2, 6).start()

    def weight_chunk(at):
        weight_recv(at // 2, 1 + at % 2)
        weight_copy(at // 2, 3 + at % 2).start()
        if at + 2 < 8:
            weight_copy((at + 2) // 2, 1 + at % 2).start()
        if at % 2 == 1:
            weight_copy(at // 2, 5).start()
        if at >= 2:
            finish_chunk(at - 2)

    def cot_copy(step):
        peer = lax.rem(z + step, count)
        return remote(mine.at[peer], cs.at[z], 52 + step, (rep, dp, peer))

    chain_send(0, 1)
    for at in range(2):
        weight_copy(0, 1 + at).start()
    for piece in range(4):
        weight_copy(piece, 0).start()
    for copy in local:
        copy.wait()

    length = length_ref[0]
    columns = [slice(at * width, (at + 1) * width) for at in range(count)]
    real = z * rows + lax.broadcasted_iota(jnp.int32, (rows, width), 0) < length
    for at in range(count):
        kept = jnp.where(real, upstream[:, columns[at]].astype(jnp.float32), 0.0)
        mine[at] = kept.astype(jnp.bfloat16)
    cs[z] = mine[z]

    for at in range(4):
        weight_chunk(at)
    chain_recv(0, 1)
    chain_send(0, 2)
    for at in range(4, 6):
        weight_chunk(at)
    for step in (0, 5, 6):
        weight_recv(0, step)
    masked = jnp.concatenate([mine[at] for at in range(count)], axis=1)
    matrix = dot(masked, wo[...].reshape(512, 1024), 1, 1).astype(jnp.bfloat16)
    for head in range(heads):
        gs[z, head] = matrix[:, head * HEAD : (head + 1) * HEAD]
    weight_chunk(6)
    chain_recv(0, 2)
    chain_send(0, 3)
    for step in range(1, count):
        cot_copy(step).start()
    chain_send(1, 1)
    weight_chunk(7)
    finish_chunk(6)
    finish_chunk(7)
    for piece in range(1, 4):
        for step in (0, 5, 6):
            weight_recv(piece, step)

    def project(block):
        inputs = xs[block]
        start = pl.multiple_of(block * rows, rows)
        for pool, kept in ((wk, ks), (wv, vs), (wq, qs)):
            matrix = dot(inputs, pool[...].reshape(1024, 512), 1, 0).astype(jnp.bfloat16)
            for head in range(heads):
                kept[head, pl.ds(start, rows), :] = matrix[:, head * HEAD : (head + 1) * HEAD]

    def project_hops(first, last):
        def body(step, carry):
            hop = step // 2
            block = z + hop * (1 - 2 * lax.rem(step, 2))

            @pl.when((block >= 0) & (block < count))
            def _():
                project(jnp.clip(block, 0, count - 1))

            return carry

        lax.fori_loop(first, last, body, 0)

    project_hops(1, 6)
    chain_recv(0, 3)
    project_hops(6, 8)

    def key_mask(amount):
        return lax.broadcasted_iota(jnp.int32, (amount, full), 1) < length

    def forward(step, carry):
        head = step // 2
        amount = full // 2
        start = pl.multiple_of(lax.rem(step, 2) * amount, amount)
        usable = key_mask(amount)
        scores = dot(qs[head, pl.ds(start, amount), :], ks[head], 1, 1) * scale
        scores = jnp.where(usable, scores, MASKED_SCORE)
        maxima = jnp.max(scores, axis=1, keepdims=True)
        exponent = jnp.exp(scores - maxima)
        totals = jnp.sum(exponent, axis=1, keepdims=True)
        mixed = dot(exponent.astype(jnp.bfloat16), vs[head], 1, 0)
        ctx[head, pl.ds(start, amount), :] = (mixed * (1.0 / totals)).astype(jnp.bfloat16)
        logsum[head, pl.ds(start, amount), :] = maxima + jnp.log(totals)
        return carry

    lax.fori_loop(0, 4, forward, 0)
    chain_recv(1, 1)
    chain_send(1, 2)
    lax.fori_loop(4, 8, forward, 0)

    own = pl.ds(pl.multiple_of(z * rows, rows), rows)
    for step in range(1, count):
        source = lax.rem(z + count - step, count)
        remote(cs.at[source], cs.at[source], 52 + step, (rep, dp, z)).wait_recv()
    masked_slice = cs[...].reshape(full, width)
    for head in range(heads):
        part[head] = dot(ctx[head], masked_slice, 0, 0).astype(jnp.bfloat16)

    def part_copy(step):
        peer = lax.rem(group + step, 8)
        peer_dp = lax.rem(peer, 4)
        return remote(part.at[peer_dp], part_in.at[step], 40 + step, (peer // 4, peer_dp, z))

    for step in range(1, 8):
        part_copy(step).start()
    chain_recv(1, 2)
    chain_send(1, 3)

    own_context = jnp.concatenate([ctx[head, own, :] for head in range(heads)], axis=1)
    attended = dot(own_context, wo[...].reshape(512, 1024), 1, 0)
    row_at = z * rows + lax.broadcasted_iota(jnp.int32, attended.shape, 0)
    attended_ref[0] = jnp.where(row_at < length, attended, 0.0).astype(jnp.bfloat16)

    total = part[dp].astype(jnp.float32)
    for step in range(1, 8):
        part_copy(step).wait_recv()
        total = total + part_in[step].astype(jnp.float32)
    slices[z] = total.astype(jnp.bfloat16)

    def slice_copy(step):
        return remote(
            slices.at[z], slices.at[z], 48 + step, (rep, dp, lax.rem(z + step, count))
        )

    for step in range(1, count):
        slice_copy(step).start()

    chain_recv(1, 3)

    def backward(head, carry):
        queries, keys, values = qs[head], ks[head], vs[head]
        grads = gs[:, head].reshape(full, HEAD)
        terms = grads.astype(jnp.float32) * ctx[head].astype(jnp.float32)
        deltas[...] = jnp.sum(terms, axis=1, keepdims=True)
        own_keys, own_values = ks[head, own, :], vs[head, own, :]
        scores = dot(queries, own_keys, 1, 1) * scale
        at = z * rows + lax.broadcasted_iota(jnp.int32, scores.shape, 1)
        attention = jnp.where(at < length, jnp.exp(scores - logsum[head]), 0.0)
        dv[head] = dot(attention.astype(jnp.bfloat16), grads, 0, 0).astype(jnp.bfloat16)
        grad_prob = dot(grads, own_values, 1, 1)
        grad_score = (attention * (grad_prob - deltas[...])).astype(jnp.bfloat16)
        dk[head] = (dot(grad_score, queries, 0, 0) * scale).astype(jnp.bfloat16)
        scores = dot(qs[head, own, :], keys, 1, 1) * scale
        attention = jnp.where(key_mask(rows), jnp.exp(scores - logsum[head, own, :]), 0.0)
        grad_prob = dot(gs[z, head], values, 1, 1)
        grad_score = (attention * (grad_prob - deltas[own, :])).astype(jnp.bfloat16)
        dq[head] = (dot(grad_score, keys, 1, 0) * scale).astype(jnp.bfloat16)
        return carry

    lax.fori_loop(0, heads, backward, 0)

    grads = [
        jnp.concatenate([kept[head] for head in range(heads)], axis=1) for kept in (dq, dk, dv)
    ]
    for shard in range(4):
        added = (
            dot(grads[0], wq[shard], 1, 1)
            + dot(grads[1], wk[shard], 1, 1)
            + dot(grads[2], wv[shard], 1, 1)
        )
        grad_frames_ref[0, :, shard * 256 : (shard + 1) * 256] = added.astype(jnp.bfloat16)

    for piece in range(4):
        for step in range(7):
            weight_copy(piece, step).wait_send()
    for which in range(2):
        for hop in range(1, count):
            for side in range(2):
                valid, copy = chain(which, side, hop)

                @pl.when(valid)
                def _():
                    copy.wait_send()

    for step in range(1, count):
        cot_copy(step).wait_send()
    for step in range(1, 8):
        part_copy(step).wait_send()
    for step in range(1, count):
        source = lax.rem(z + count - step, count)
        remote(slices.at[source], slices.at[source], 48 + step, (rep, dp, z)).wait_recv()
    for step in range(1, count):
        slice_copy(step).wait_send()
    for at in range(count):
        grad_out_ref[:, at * width : (at + 1) * width] = slices[at].astype(jnp.float32)


def fused(frames, lengths, cotangent, w_query, w_key, w_value, w_out):
    vmem = pl.BlockSpec(memory_space=pltpu.VMEM)
    hbm = pl.BlockSpec(memory_space=pltpu.HBM)
    bf16, f32 = jnp.bfloat16, jnp.float32
    per_head = pltpu.VMEM((4, 512, HEAD), bf16)
    own_head = pltpu.VMEM((4, 128, HEAD), bf16)
    return pl.pallas_call(
        fused_kernel,
        out_shape=(
            jax.ShapeDtypeStruct(frames.shape, bf16),
            jax.ShapeDtypeStruct(frames.shape, bf16),
            jax.ShapeDtypeStruct(w_out.shape, f32),
        ),
        in_specs=[hbm, pl.BlockSpec(memory_space=pltpu.SMEM)] + [hbm] * 5,
        out_specs=(vmem, vmem, vmem),
        scratch_shapes=[
            pltpu.VMEM((4, 128, 1024), bf16),
            pltpu.VMEM((128, 1024), bf16),
            pltpu.VMEM((4, 128, 256), bf16),
            pltpu.VMEM((4, 128, 256), bf16),
            pltpu.VMEM((4, 256, 512), bf16),
            pltpu.VMEM((4, 256, 512), bf16),
            pltpu.VMEM((4, 256, 512), bf16),
            pltpu.VMEM((4, 128, 1024), bf16),
            per_head,
            per_head,
            per_head,
            pltpu.VMEM((4, 4, 128, HEAD), bf16),
            per_head,
            pltpu.VMEM((4, 512, 1), f32),
            pltpu.VMEM((512, 1), f32),
            own_head,
            own_head,
            own_head,
            pltpu.VMEM((4, 128, 256), bf16),
            pltpu.VMEM((8, 128, 256), bf16),
            pltpu.VMEM((4, 128, 256), bf16),
            pltpu.SemaphoreType.DMA((56,)),
            pltpu.SemaphoreType.DMA((56,)),
            pltpu.SemaphoreType.DMA((6,)),
        ],
        compiler_params=pltpu.CompilerParams(
            collective_id=0, has_side_effects=True, vmem_limit_bytes=48 * 1024 * 1024
        ),
    )(frames, lengths, cotangent, w_query, w_key, w_value, w_out)


def either(sizes, frames, lengths, cotangent, w_query, w_key, w_value, w_out):
    fits = sizes == (2, 4, 4) and frames.shape == (1, 128, 1024) and w_query.shape == (256, 512)
    chosen = fused if fits else shards
    return chosen(frames, lengths, cotangent, w_query, w_key, w_value, w_out)


def solution(mesh):
    in_specs = (
        P(("rep", "dp"), "ctx", None),
        P(("rep", "dp")),
        P(("rep", "dp"), "ctx", None),
        P("dp", None),
        P("dp", None),
        P("dp", None),
        P("dp", None),
    )
    out_specs = (P(("rep", "dp"), "ctx", None), P(("rep", "dp"), "ctx", None), P("dp", None))
    sizes = (mesh.shape["rep"], mesh.shape["dp"], mesh.shape["ctx"])
    body = functools.partial(either, sizes)
    return jax.shard_map(body, mesh=mesh, in_specs=in_specs, out_specs=out_specs, check_vma=False)
```

profile of v0, /device:TPU:29, one launch (start us, length us, event | category | flops | bytes accessed | tf_op | source)
XLA Modules:
  0.0 56.3 jit_solution(9465885220809049777)
XLA Ops:
  1.3 0.0 copy-start
  1.3 0.9 %copy-done = bf16[1,128,1024]{2,1,0:T(8,128)(2,1)S(1)} copy-done((bf16[1,128,1024]{2,1,0:T(8,128)(2,1)S(1)}, bf16[1,128,1024]{2,1,0:T(8,128)(2,1)}, u32[]{:S(2)}) %copy-start) | copy-done | bytes 262168
  2.2 0.0 copy-start.1
  2.2 0.9 %copy-done.1 = bf16[1,128,1024]{2,1,0:T(8,128)(2,1)S(1)} copy-done((bf16[1,128,1024]{2,1,0:T(8,128)(2,1)S(1)}, bf16[1,128,1024]{2,1,0:T(8,128)(2,1)}, u32[]{:S(2)}) %copy-start.1) | copy-done | bytes 262168
  3.2 0.0 copy-start.2
  3.2 0.9 %copy-done.2 = bf16[256,512]{1,0:T(8,128)(2,1)S(1)} copy-done((bf16[256,512]{1,0:T(8,128)(2,1)S(1)}, bf16[256,512]{1,0:T(8,128)(2,1)}, u32[]{:S(2)}) %copy-start.2) | copy-done | bytes 262168
  4.1 0.0 copy-start.3
  4.1 0.9 %copy-done.3 = bf16[256,512]{1,0:T(8,128)(2,1)S(1)} copy-done((bf16[256,512]{1,0:T(8,128)(2,1)S(1)}, bf16[256,512]{1,0:T(8,128)(2,1)}, u32[]{:S(2)}) %copy-start.3) | copy-done | bytes 262168
  5.1 0.0 copy-start.4
  5.1 0.9 %copy-done.4 = bf16[256,512]{1,0:T(8,128)(2,1)S(1)} copy-done((bf16[256,512]{1,0:T(8,128)(2,1)S(1)}, bf16[256,512]{1,0:T(8,128)(2,1)}, u32[]{:S(2)}) %copy-start.4) | copy-done | bytes 262168
  6.0 0.0 copy-start.5
  6.0 0.9 %copy-done.5 = bf16[128,1024]{1,0:T(8,128)(2,1)S(1)} copy-done((bf16[128,1024]{1,0:T(8,128)(2,1)S(1)}, bf16[128,1024]{1,0:T(8,128)(2,1)}, u32[]{:S(2)}) %copy-start.5) | copy-done | bytes 262168
  7.0 47.1 %shard_map.94 = (bf16[1,128,1024]{2,1,0:T(8,128)(2,1)S(1)}, bf16[1,128,1024]{2,1,0:T(8,128)(2,1)S(1)}, f32[128,1024]{1,0:T(8,128)S(1)}) custom-call(bf16[1,128,1024]{2,1,0:T(8,128)(2,1)S(1)} %copy-done, s32[1]{0:T(128)S(6)} %copy.13.length_ref, bf16[1,128,1024]{2,1,0:T(8,128)(2,1)S(1)} %copy-done.1, bf16[256,512]{1,0:T(8,128)(2,1)S(1)} %copy-done.2, ...), custom_call_target="tpu_custom_call" | custom-call | tf_op jit(solution)/shard_map/pallas_call | solution.py:612
  54.1 0.7 %copy.14 = bf16[1,128,1024]{2,1,0:T(8,128)(2,1)} copy(bf16[1,128,1024]{2,1,0:T(8,128)(2,1)S(1)} %get-tuple-element.6) | data formatting | bytes 524288
  54.8 0.7 %copy.15 = bf16[1,128,1024]{2,1,0:T(8,128)(2,1)} copy(bf16[1,128,1024]{2,1,0:T(8,128)(2,1)S(1)} %get-tuple-element.7) | data formatting | bytes 524288
  55.5 0.8 %copy.16 = f32[128,1024]{1,0:T(8,128)} copy(f32[128,1024]{1,0:T(8,128)S(1)} %get-tuple-element.8) | data formatting | bytes 1048576
Async XLA Ops:
  1.3 1.0 %copy-start = (bf16[1,128,1024]{2,1,0:T(8,128)(2,1)S(1)}, bf16[1,128,1024]{2,1,0:T(8,128)(2,1)}, u32[]{:S(2)}) copy-start(bf16[1,128,1024]{2,1,0:T(8,128)(2,1)} %frames_ref.1) | copy-start | bytes 786436
  2.2 0.9 %copy-start.1 = (bf16[1,128,1024]{2,1,0:T(8,128)(2,1)S(1)}, bf16[1,128,1024]{2,1,0:T(8,128)(2,1)}, u32[]{:S(2)}) copy-start(bf16[1,128,1024]{2,1,0:T(8,128)(2,1)} %cot_ref.1) | copy-start | bytes 786436
  3.2 0.9 %copy-start.2 = (bf16[256,512]{1,0:T(8,128)(2,1)S(1)}, bf16[256,512]{1,0:T(8,128)(2,1)}, u32[]{:S(2)}) copy-start(bf16[256,512]{1,0:T(8,128)(2,1)} %wq_ref.1) | copy-start | bytes 786436
  4.1 0.9 %copy-start.3 = (bf16[256,512]{1,0:T(8,128)(2,1)S(1)}, bf16[256,512]{1,0:T(8,128)(2,1)}, u32[]{:S(2)}) copy-start(bf16[256,512]{1,0:T(8,128)(2,1)} %wk_ref.1) | copy-start | bytes 786436
  5.1 0.9 %copy-start.4 = (bf16[256,512]{1,0:T(8,128)(2,1)S(1)}, bf16[256,512]{1,0:T(8,128)(2,1)}, u32[]{:S(2)}) copy-start(bf16[256,512]{1,0:T(8,128)(2,1)} %wv_ref.1) | copy-start | bytes 786436
  6.0 0.9 %copy-start.5 = (bf16[128,1024]{1,0:T(8,128)(2,1)S(1)}, bf16[128,1024]{1,0:T(8,128)(2,1)}, u32[]{:S(2)}) copy-start(bf16[128,1024]{1,0:T(8,128)(2,1)} %wo_ref.1) | copy-start | bytes 786436
where the time goes:
time: 56.6 us; the launch traced here: 56.3 us
  Pallas kernels  47.1 us (83%)
  local copies, waits for them, and re-layouts  7.89 us (14%)
  between operations  1.3 us (2%)
    pallas_call x1, Pallas kernels, fused(): pl.pallas_call(fused_kernel, out_shape=(jax.ShapeDtypeStruct(frames.shape...  47.1 us
    unnamed x15, local copies, waits for them, and re-layouts  7.89 us

commit v1 on v0

--- a/solution.py
+++ b/solution.py
@@ -645,7 +645,7 @@
             pltpu.SemaphoreType.DMA((6,)),
         ],
         compiler_params=pltpu.CompilerParams(
-            collective_id=0, has_side_effects=True, vmem_limit_bytes=48 * 1024 * 1024
+            collective_id=0, has_side_effects=True, vmem_limit_bytes=56 * 1024 * 1024
         ),
     )(frames, lengths, cotangent, w_query, w_key, w_value, w_out)
 

time: 56.6 us -> 52.6 us (0.929)
  the two profiles are of different devices: /device:TPU:29 before, /device:TPU:0 now
where the time goes in v1:
time: 52.6 us; the launch traced here: 52.4 us
  Pallas kernels  47.9 us (91%)
  local copies, waits for them, and re-layouts  3.24 us (6%)
  between operations  1.3 us (2%)
    pallas_call x1, Pallas kernels, fused(): pl.pallas_call(fused_kernel, out_shape=(jax.ShapeDtypeStruct(frames.shape...  47.9 us
    unnamed x7, local copies, waits for them, and re-layouts  3.24 us

profile of v1, /device:TPU:0, one launch (start us, length us, event | category | flops | bytes accessed | tf_op | source)
XLA Modules:
  0.0 52.4 jit_solution(17161678171213965842)
XLA Ops:
  1.3 47.9 %shard_map.94 = (bf16[1,128,1024]{2,1,0:T(8,128)(2,1)}, bf16[1,128,1024]{2,1,0:T(8,128)(2,1)}, f32[128,1024]{1,0:T(8,128)}) custom-call(bf16[1,128,1024]{2,1,0:T(8,128)(2,1)} %frames_ref.1, s32[1]{0:T(128)S(6)} %copy.13.length_ref, bf16[1,128,1024]{2,1,0:T(8,128)(2,1)} %cot_ref.1, bf16[256,512]{1,0:T(8,128)(2,1)} %wq_ref.1, bf16[256,512]{1,0:T(8,128)(2,1)} %wk_ref.1, ...), custom_call_target="tpu_custom_call" | custom-call | tf_op jit(solution)/shard_map/pallas_call | solution.py:612
  49.2 0.0 copy-start.1
  49.2 0.0 copy-start
  49.2 1.7 %copy.14 = bf16[1,128,1024]{2,1,0:T(8,128)(2,1)} copy(bf16[1,128,1024]{2,1,0:T(8,128)(2,1)} %get-tuple-element.6) | data formatting | bytes 524288
  50.9 0.0 copy-done.1
  50.9 0.7 %copy.15 = bf16[1,128,1024]{2,1,0:T(8,128)(2,1)} copy(bf16[1,128,1024]{2,1,0:T(8,128)(2,1)S(1)} %copy-done.1) | data formatting | bytes 524288
  51.6 0.0 copy-done
  51.6 0.8 %copy.16 = f32[128,1024]{1,0:T(8,128)} copy(f32[128,1024]{1,0:T(8,128)S(1)} %copy-done) | data formatting | bytes 1048576
Async XLA Ops:
  49.2 1.8 %copy-start.1 = (bf16[1,128,1024]{2,1,0:T(8,128)(2,1)S(1)}, bf16[1,128,1024]{2,1,0:T(8,128)(2,1)}, u32[]{:S(2)}) copy-start(bf16[1,128,1024]{2,1,0:T(8,128)(2,1)} %get-tuple-element.7) | copy-start | bytes 786436
  49.2 2.5 %copy-start = (f32[128,1024]{1,0:T(8,128)S(1)}, f32[128,1024]{1,0:T(8,128)}, u32[]{:S(2)}) copy-start(f32[128,1024]{1,0:T(8,128)} %get-tuple-element.8) | copy-start | bytes 1572868

commit v2 on v1

--- a/solution.py
+++ b/solution.py
@@ -283,24 +283,26 @@
     heads = 4
     rows = frames_ref.shape[1]
     full = rows * count
-    width = slices.shape[2]
     scale = HEAD ** (-0.5)
     sibling = dp + 1 - 2 * lax.rem(dp, 2)
     across = lax.rem(dp + 2, 4)
     across_sibling = lax.rem(sibling + 2, 4)
     other_rep = 1 - rep
     group = rep * 4 + dp
+    lower = z < 2
+    middle = (z == 1) | (z == 2)
+    side_at = jnp.clip(z - 1, 0, 1)
 
     local = [
         pltpu.make_async_copy(source, target, local_sem.at[at])
         for at, (source, target) in enumerate(
             (
+                (cot_ref.at[0], upstream),
+                (frames_ref.at[0], xs.at[z]),
                 (wk_ref, wk.at[dp]),
                 (wv_ref, wv.at[dp]),
                 (wq_ref, wq.at[dp]),
                 (wo_ref, wo.at[dp]),
-                (frames_ref.at[0], xs.at[z]),
-                (cot_ref.at[0], upstream),
             )
         )
     ]
@@ -309,58 +311,75 @@
 
     barrier = pltpu.get_barrier_semaphore()
     for step in range(1, count):
-        pl.semaphore_signal(
-            barrier, inc=1, device_id=(rep, dp, lax.rem(z + step, count)), device_id_type=MESH
-        )
+        for to_rep in (rep, other_rep):
+            pl.semaphore_signal(
+                barrier,
+                inc=1,
+                device_id=(to_rep, dp, lax.rem(z + step, count)),
+                device_id_type=MESH,
+            )
     for step in range(1, 8):
         peer = lax.rem(group + step, 8)
         pl.semaphore_signal(
             barrier, inc=1, device_id=(peer // 4, lax.rem(peer, 4), z), device_id_type=MESH
         )
-    pl.semaphore_wait(barrier, 10)
-
-    def remote(source, target, index, device):
+    pl.semaphore_wait(barrier, 13)
+
+    def remote(source, target, sent, received, device):
         return pltpu.make_async_remote_copy(
             src_ref=source,
             dst_ref=target,
-            send_sem=send_sem.at[index],
-            recv_sem=recv_sem.at[index],
+            send_sem=send_sem.at[sent],
+            recv_sem=recv_sem.at[received],
             device_id=device,
             device_id_type=MESH,
         )
 
-    def chain(which, side, hop):
+    def arrive(target, received):
+        remote(target, target, received, received, (rep, dp, z)).wait_recv()
+
+    def piece_of(which, slot, at):
+        if which == 0:
+            return xs.at[slot, pl.ds(at * (rows // 2), rows // 2)]
+        return gs.at[slot, pl.ds(at * 2, 2)]
+
+    def chain(which, side, hop, at):
         sign = 1 - 2 * side
-        pool = (xs, gs)[which]
         owner = z - sign * (hop - 1)
         slot = jnp.clip(owner, 0, count - 1)
-        source = frames_ref.at[0] if which == 0 and hop == 1 else pool.at[slot]
+        source = piece_of(which, slot, at)
+        if which == 0 and hop == 1:
+            source = frames_ref.at[0, pl.ds(at * (rows // 2), rows // 2)]
         target = jnp.clip(z + sign, 0, count - 1)
-        index = which * 6 + side * 3 + hop - 1
+        index = which * 12 + side * 6 + (hop - 1) * 2 + at
         valid = (z + sign >= 0) & (z + sign < count) & (owner >= 0) & (owner < count)
-        return valid, remote(source, pool.at[slot], index, (rep, dp, target))
-
-    def chain_send(which, hop):
+        copy = remote(source, piece_of(which, slot, at), index, index, (rep, dp, target))
+        return valid, copy
+
+    def chain_send(which, hop, at):
         for side in range(2):
-            valid, copy = chain(which, side, hop)
+            valid, copy = chain(which, side, hop, at)
 
             @pl.when(valid)
             def _():
                 copy.start()
 
-    def chain_recv(which, hop):
+    def chain_recv(which, hop, at):
         for side in range(2):
-            sign = 1 - 2 * side
-            pool = (xs, gs)[which]
-            owner = z - sign * hop
+            owner = z - (1 - 2 * side) * hop
             slot = jnp.clip(owner, 0, count - 1)
-            index = which * 6 + side * 3 + hop - 1
+            index = which * 12 + side * 6 + (hop - 1) * 2 + at
 
             @pl.when((owner >= 0) & (owner < count))
             def _():
-                remote(pool.at[slot], pool.at[slot], index, (rep, dp, z)).wait_recv()
-
-    weights = ((wo_ref, wo), (wk_ref, wk), (wv_ref, wv), (wq_ref, wq))
+                arrive(piece_of(which, slot, at), index)
+
+    def chain_pass(which, hop, at):
+        chain_recv(which, hop, at)
+        if hop < 3:
+            chain_send(which, hop + 1, at)
+
+    weights = ((wk_ref, wk), (wv_ref, wv), (wq_ref, wq), (wo_ref, wo))
 
     def half(ref, which):
         size = ref.shape[0] // 2
@@ -372,22 +391,21 @@
 
     def weight_copy(piece, step):
         shard, pool = weights[piece]
-        index = 12 + piece * 7 + step
+        index = 24 + piece * 7 + step
         if step == 0:
-            return remote(shard, pool.at[dp], index, (rep, sibling, z))
+            return remote(shard, pool.at[dp], index, index, (rep, sibling, z))
         if step < 3:
             target = chunk(pool.at[dp], rep, step - 1)
-            return remote(chunk(shard, rep, step - 1), target, index, (rep, across, z))
+            return remote(chunk(shard, rep, step - 1), target, index, index, (rep, across, z))
         mine_at = pool.at[across]
         if step < 5:
             source = chunk(mine_at, rep, step - 3)
-            return remote(source, source, index, (other_rep, dp, z))
+            return remote(source, source, index, index, (other_rep, dp, z))
         source = half(mine_at, rep if step == 5 else other_rep)
-        return remote(source, source, index, (rep, sibling, z))
+        return remote(source, source, index, index, (rep, sibling, z))
 
     def weight_recv(piece, step):
         pool = weights[piece][1]
-        index = 12 + piece * 7 + step
         if step == 0:
             target = pool.at[sibling]
         elif step < 3:
@@ -396,154 +414,182 @@
             target = chunk(pool.at[across], other_rep, step - 3)
         else:
             target = half(pool.at[across_sibling], rep if step == 5 else other_rep)
-        remote(target, target, index, (rep, dp, z)).wait_recv()
-
-    def finish_chunk(at):
+        arrive(target, 24 + piece * 7 + step)
+
+    def from_y(at):
+        weight_recv(at // 2, 1 + at % 2)
+        weight_copy(at // 2, 3 + at % 2).start()
+        if at % 2 == 1:
+            weight_copy(at // 2, 5).start()
+
+    def from_x(at):
         weight_recv(at // 2, 3 + at % 2)
         if at % 2 == 1:
             weight_copy(at // 2, 6).start()
 
-    def weight_chunk(at):
-        weight_recv(at // 2, 1 + at % 2)
-        weight_copy(at // 2, 3 + at % 2).start()
-        if at + 2 < 8:
-            weight_copy((at + 2) // 2, 1 + at % 2).start()
-        if at % 2 == 1:
-            weight_copy(at // 2, 5).start()
-        if at >= 2:
-            finish_chunk(at - 2)
-
-    def cot_copy(step):
-        peer = lax.rem(z + step, count)
-        return remote(mine.at[peer], cs.at[z], 52 + step, (rep, dp, peer))
-
-    chain_send(0, 1)
+    def cot_copy(near):
+        to = jnp.where(lower, 1, 2) if near else jnp.where(lower, 2, 1)
+        sent = 52 + (0 if near else 1)
+        return remote(mine.at[to - 1], cs.at[z], sent, 52 + z, (rep, dp, to))
+
     for at in range(2):
-        weight_copy(0, 1 + at).start()
+        chain_send(0, 1, at)
+    for piece in range(4):
+        for step in (1, 2):
+            weight_copy(piece, step).start()
     for piece in range(4):
         weight_copy(piece, 0).start()
     for copy in local:
         copy.wait()
 
     length = length_ref[0]
-    columns = [slice(at * width, (at + 1) * width) for at in range(count)]
+    width = mine.shape[2]
     real = z * rows + lax.broadcasted_iota(jnp.int32, (rows, width), 0) < length
-    for at in range(count):
-        kept = jnp.where(real, upstream[:, columns[at]].astype(jnp.float32), 0.0)
-        mine[at] = kept.astype(jnp.bfloat16)
-    cs[z] = mine[z]
-
-    for at in range(4):
-        weight_chunk(at)
-    chain_recv(0, 1)
-    chain_send(0, 2)
-    for at in range(4, 6):
-        weight_chunk(at)
+    for at in range(2):
+        kept = upstream[:, at * width : (at + 1) * width].astype(jnp.float32)
+        mine[at] = jnp.where(real, kept, 0.0).astype(jnp.bfloat16)
+    cs[z] = mine[side_at]
+
+    from_y(0)
+    from_y(1)
+    chain_pass(0, 1, 0)
+    from_y(2)
+    from_x(0)
+    from_y(3)
+    chain_pass(0, 1, 1)
+
+    @pl.when(jnp.logical_not(middle))
+    def _():
+        cot_copy(True).start()
+
+    cot_copy(False).start()
+    from_x(1)
+    from_y(4)
+    from_x(2)
+    from_y(5)
+    chain_pass(0, 2, 0)
+    from_x(3)
+    from_y(6)
+    from_x(4)
+    from_y(7)
+    chain_pass(0, 2, 1)
+    from_x(5)
+    for piece in range(3):
+        for step in (0, 5, 6):
+            weight_recv(piece, step)
+
+    def project(first, blocks):
+        inputs = xs[pl.ds(first, blocks)].reshape(blocks * rows, 1024)
+        start = pl.multiple_of(first * rows, rows)
+        for pool, kept in ((wk, ks), (wv, vs), (wq, qs)):
+            matrix = dot(inputs, pool[...].reshape(1024, 512), 1, 0).astype(jnp.bfloat16)
+            for head in range(heads):
+                kept[head, pl.ds(start, blocks * rows), :] = matrix[
+                    :, head * HEAD : (head + 1) * HEAD
+                ]
+
+    project(jnp.where(lower, 0, 1), 3)
+    from_x(6)
+    from_x(7)
     for step in (0, 5, 6):
-        weight_recv(0, step)
-    masked = jnp.concatenate([mine[at] for at in range(count)], axis=1)
+        weight_recv(3, step)
+    masked = jnp.concatenate([mine[0], mine[1]], axis=1)
     matrix = dot(masked, wo[...].reshape(512, 1024), 1, 1).astype(jnp.bfloat16)
     for head in range(heads):
         gs[z, head] = matrix[:, head * HEAD : (head + 1) * HEAD]
-    weight_chunk(6)
-    chain_recv(0, 2)
-    chain_send(0, 3)
-    for step in range(1, count):
-        cot_copy(step).start()
-    chain_send(1, 1)
-    weight_chunk(7)
-    finish_chunk(6)
-    finish_chunk(7)
-    for piece in range(1, 4):
-        for step in (0, 5, 6):
-            weight_recv(piece, step)
-
-    def project(block):
-        inputs = xs[block]
-        start = pl.multiple_of(block * rows, rows)
-        for pool, kept in ((wk, ks), (wv, vs), (wq, qs)):
-            matrix = dot(inputs, pool[...].reshape(1024, 512), 1, 0).astype(jnp.bfloat16)
-            for head in range(heads):
-                kept[head, pl.ds(start, rows), :] = matrix[:, head * HEAD : (head + 1) * HEAD]
-
-    def project_hops(first, last):
-        def body(step, carry):
-            hop = step // 2
-            block = z + hop * (1 - 2 * lax.rem(step, 2))
-
-            @pl.when((block >= 0) & (block < count))
-            def _():
-                project(jnp.clip(block, 0, count - 1))
-
-            return carry
-
-        lax.fori_loop(first, last, body, 0)
-
-    project_hops(1, 6)
-    chain_recv(0, 3)
-    project_hops(6, 8)
+    for at in range(2):
+        chain_send(1, 1, at)
+    for at in range(2):
+        chain_pass(0, 3, at)
+    project(jnp.where(lower, 3, 0), 1)
 
     def key_mask(amount):
         return lax.broadcasted_iota(jnp.int32, (amount, full), 1) < length
 
-    def forward(step, carry):
-        head = step // 2
+    def part_copy(order, head, turned):
+        to_rep = other_rep if turned else rep
+        index = order * 2 + turned
+        return remote(
+            part.at[head, to_rep], part_in.at[index], 56 + index, 56 + index, (to_rep, head, z)
+        )
+
+    def forward(order, carry):
+        head = lax.rem(dp + lax.rem(order, 2) * (sibling - dp) + 2 * (1 - order // 2) + 4, 4)
         amount = full // 2
-        start = pl.multiple_of(lax.rem(step, 2) * amount, amount)
         usable = key_mask(amount)
-        scores = dot(qs[head, pl.ds(start, amount), :], ks[head], 1, 1) * scale
-        scores = jnp.where(usable, scores, MASKED_SCORE)
-        maxima = jnp.max(scores, axis=1, keepdims=True)
-        exponent = jnp.exp(scores - maxima)
-        totals = jnp.sum(exponent, axis=1, keepdims=True)
-        mixed = dot(exponent.astype(jnp.bfloat16), vs[head], 1, 0)
-        ctx[head, pl.ds(start, amount), :] = (mixed * (1.0 / totals)).astype(jnp.bfloat16)
-        logsum[head, pl.ds(start, amount), :] = maxima + jnp.log(totals)
+        for at in range(2):
+            start = at * amount
+            scores = dot(qs[head, pl.ds(start, amount), :], ks[head], 1, 1) * scale
+            scores = jnp.where(usable, scores, MASKED_SCORE)
+            maxima = jnp.max(scores, axis=1, keepdims=True)
+            exponent = jnp.exp(scores - maxima)
+            totals = jnp.sum(exponent, axis=1, keepdims=True)
+            mixed = dot(exponent.astype(jnp.bfloat16), vs[head], 1, 0)
+            ctx[head, pl.ds(start, amount), :] = (mixed * (1.0 / totals)).astype(jnp.bfloat16)
+            logsum[head, pl.ds(start, amount), :] = maxima + jnp.log(totals)
+
+        @pl.when(middle)
+        def _():
+            @pl.when(order == 0)
+            def _():
+                for source in range(count):
+
+                    @pl.when(z != source)
+                    def _():
+                        arrive(cs.at[source], 52 + source)
+
+            product = dot(ctx[head], cs[...].reshape(full, width), 0, 0)
+            for at in range(2):
+                part[head, at] = product[:, at * 256 : (at + 1) * 256].astype(jnp.bfloat16)
+
+            @pl.when(order != 2)
+            def _():
+                part_copy(order, head, 0).start()
+
+            part_copy(order, head, 1).start()
+
         return carry
 
-    lax.fori_loop(0, 4, forward, 0)
-    chain_recv(1, 1)
-    chain_send(1, 2)
-    lax.fori_loop(4, 8, forward, 0)
-
+    lax.fori_loop(0, heads, forward, 0)
+
+    for at in range(2):
+        chain_pass(1, 1, at)
     own = pl.ds(pl.multiple_of(z * rows, rows), rows)
-    for step in range(1, count):
-        source = lax.rem(z + count - step, count)
-        remote(cs.at[source], cs.at[source], 52 + step, (rep, dp, z)).wait_recv()
-    masked_slice = cs[...].reshape(full, width)
-    for head in range(heads):
-        part[head] = dot(ctx[head], masked_slice, 0, 0).astype(jnp.bfloat16)
-
-    def part_copy(step):
-        peer = lax.rem(group + step, 8)
-        peer_dp = lax.rem(peer, 4)
-        return remote(part.at[peer_dp], part_in.at[step], 40 + step, (peer // 4, peer_dp, z))
-
-    for step in range(1, 8):
-        part_copy(step).start()
-    chain_recv(1, 2)
-    chain_send(1, 3)
-
     own_context = jnp.concatenate([ctx[head, own, :] for head in range(heads)], axis=1)
     attended = dot(own_context, wo[...].reshape(512, 1024), 1, 0)
     row_at = z * rows + lax.broadcasted_iota(jnp.int32, attended.shape, 0)
     attended_ref[0] = jnp.where(row_at < length, attended, 0.0).astype(jnp.bfloat16)
-
-    total = part[dp].astype(jnp.float32)
-    for step in range(1, 8):
-        part_copy(step).wait_recv()
-        total = total + part_in[step].astype(jnp.float32)
-    slices[z] = total.astype(jnp.bfloat16)
-
-    def slice_copy(step):
+    for at in range(2):
+        chain_pass(1, 2, at)
+
+    mine_slice = side_at * 2 + rep
+
+    def slice_copy(step, turned):
+        to_rep = other_rep if turned else rep
+        block = slices.at[mine_slice]
         return remote(
-            slices.at[z], slices.at[z], 48 + step, (rep, dp, lax.rem(z + step, count))
+            block,
+            block,
+            64 + step * 2 + turned,
+            64 + mine_slice,
+            (to_rep, dp, lax.rem(z + step, count)),
         )
 
-    for step in range(1, count):
-        slice_copy(step).start()
-
-    chain_recv(1, 3)
+    @pl.when(middle)
+    def _():
+        total = part[dp, rep].astype(jnp.float32)
+        for index in range(8):
+            if index != 4:
+                arrive(part_in.at[index], 56 + index)
+                total = total + part_in[index].astype(jnp.float32)
+        slices[mine_slice] = total.astype(jnp.bfloat16)
+        for step in (1, 3, 2, 0):
+            for turned in range(2):
+                if step + turned > 0:
+                    slice_copy(step, turned).start()
+
+    for at in range(2):
+        chain_pass(1, 3, at)
 
     def backward(head, carry):
         queries, keys, values = qs[head], ks[head], vs[head]
@@ -583,24 +629,50 @@
             weight_copy(piece, step).wait_send()
     for which in range(2):
         for hop in range(1, count):
-            for side in range(2):
-                valid, copy = chain(which, side, hop)
-
-                @pl.when(valid)
-                def _():
-                    copy.wait_send()
-
-    for step in range(1, count):
-        cot_copy(step).wait_send()
-    for step in range(1, 8):
-        part_copy(step).wait_send()
-    for step in range(1, count):
-        source = lax.rem(z + count - step, count)
-        remote(slices.at[source], slices.at[source], 48 + step, (rep, dp, z)).wait_recv()
-    for step in range(1, count):
-        slice_copy(step).wait_send()
+            for at in range(2):
+                for side in range(2):
+                    valid, copy = chain(which, side, hop, at)
+
+                    @pl.when(valid)
+                    def _():
+                        copy.wait_send()
+
+    @pl.when(jnp.logical_not(middle))
+    def _():
+        cot_copy(True).wait_send()
+
+    cot_copy(False).wait_send()
+
+    @pl.when(middle)
+    def _():
+        for index in range(8):
+            if index != 4:
+                part_copy(index // 2, dp, index % 2).wait_send()
+
     for at in range(count):
-        grad_out_ref[:, at * width : (at + 1) * width] = slices[at].astype(jnp.float32)
+
+        @pl.when(jnp.logical_not(middle & (mine_slice == at)))
+        def _():
+            arrive(slices.at[at], 64 + at)
+
+    @pl.when(middle)
+    def _():
+        for step in range(count):
+            for turned in range(2):
+                if step + turned > 0:
+                    slice_copy(step, turned).wait_send()
+
+    for at in range(count):
+        grad_out_ref[:, at * 256 : (at + 1) * 256] = slices[at].astype(jnp.float32)
+
+
+def write_kernel(*refs):
+    sems = refs[6]
+    copies = [pltpu.make_async_copy(refs[at], refs[at + 3], sems.at[at]) for at in range(3)]
+    for copy in copies:
+        copy.start()
+    for copy in copies:
+        copy.wait()
 
 
 def fused(frames, lengths, cotangent, w_query, w_key, w_value, w_out):
@@ -609,20 +681,20 @@
     bf16, f32 = jnp.bfloat16, jnp.float32
     per_head = pltpu.VMEM((4, 512, HEAD), bf16)
     own_head = pltpu.VMEM((4, 128, HEAD), bf16)
-    return pl.pallas_call(
+    results = pl.pallas_call(
         fused_kernel,
         out_shape=(
-            jax.ShapeDtypeStruct(frames.shape, bf16),
-            jax.ShapeDtypeStruct(frames.shape, bf16),
-            jax.ShapeDtypeStruct(w_out.shape, f32),
+            pltpu.VMEM(frames.shape, bf16),
+            pltpu.VMEM(frames.shape, bf16),
+            pltpu.VMEM(w_out.shape, f32),
         ),
         in_specs=[hbm, pl.BlockSpec(memory_space=pltpu.SMEM)] + [hbm] * 5,
         out_specs=(vmem, vmem, vmem),
         scratch_shapes=[
             pltpu.VMEM((4, 128, 1024), bf16),
             pltpu.VMEM((128, 1024), bf16),
-            pltpu.VMEM((4, 128, 256), bf16),
-            pltpu.VMEM((4, 128, 256), bf16),
+            pltpu.VMEM((2, 128, 512), bf16),
+            pltpu.VMEM((4, 128, 512), bf16),
             pltpu.VMEM((4, 256, 512), bf16),
             pltpu.VMEM((4, 256, 512), bf16),
             pltpu.VMEM((4, 256, 512), bf16),
@@ -637,17 +709,25 @@
             own_head,
             own_head,
             own_head,
-            pltpu.VMEM((4, 128, 256), bf16),
+            pltpu.VMEM((4, 2, 128, 256), bf16),
             pltpu.VMEM((8, 128, 256), bf16),
             pltpu.VMEM((4, 128, 256), bf16),
-            pltpu.SemaphoreType.DMA((56,)),
-            pltpu.SemaphoreType.DMA((56,)),
+            pltpu.SemaphoreType.DMA((72,)),
+            pltpu.SemaphoreType.DMA((72,)),
             pltpu.SemaphoreType.DMA((6,)),
         ],
         compiler_params=pltpu.CompilerParams(
             collective_id=0, has_side_effects=True, vmem_limit_bytes=56 * 1024 * 1024
         ),
     )(frames, lengths, cotangent, w_query, w_key, w_value, w_out)
+    return pl.pallas_call(
+        write_kernel,
+        out_shape=tuple(jax.ShapeDtypeStruct(r.shape, r.dtype) for r in results),
+        in_specs=[vmem] * 3,
+        out_specs=(hbm, hbm, hbm),
+        scratch_shapes=[pltpu.SemaphoreType.DMA((3,))],
+        compiler_params=pltpu.CompilerParams(vmem_limit_bytes=4 * 1024 * 1024),
+    )(*results)
 
 
 def either(sizes, frames, lengths, cotangent, w_query, w_key, w_value, w_out):

time: 52.6 us -> 48.5 us (0.922)
  local copies, waits for them, and re-layouts: 3.24 us -> 0 us
  Pallas kernels: 47.9 us -> 47 us
    unnamed x7 -> x0, local copies, waits for them, and re-layouts: 3.24 us -> none
    pallas_call x1 -> x2, Pallas kernels: 47.9 us -> 47 us  [the longest x1 46 us: fused(): pl.pallas_call(fused_kernel, out_shape=(pltpu.VMEM(frames.shape, bf16), p...]
where the time goes in v2:
time: 48.5 us; the launch traced here: 48.3 us
  Pallas kernels  47 us (97%)
  between operations  1.29 us (3%)
    pallas_call x1, Pallas kernels, fused(): pl.pallas_call(fused_kernel, out_shape=(pltpu.VMEM(frames.shape, bf16), p...  46 us
    pallas_call x1, Pallas kernels, fused(): pl.pallas_call(write_kernel, out_shape=tuple((jax.ShapeDtypeStruct(r.shap...  0.99 us

profile of v2, /device:TPU:0, one launch (start us, length us, event | category | flops | bytes accessed | tf_op | source)
XLA Modules:
  0.0 48.3 jit_solution(8775366875204320141)
XLA Ops:
  1.3 46.0 %shard_map.94 = (bf16[1,128,1024]{2,1,0:T(8,128)(2,1)S(1)}, bf16[1,128,1024]{2,1,0:T(8,128)(2,1)S(1)}, f32[128,1024]{1,0:T(8,128)S(1)}) custom-call(bf16[1,128,1024]{2,1,0:T(8,128)(2,1)} %frames_ref.1, s32[1]{0:T(128)S(6)} %copy.10.length_ref, bf16[1,128,1024]{2,1,0:T(8,128)(2,1)} %cot_ref.1, bf16[256,512]{1,0:T(8,128)(2,1)} %wq_ref.1, ...), custom_call_target="tpu_custom_call" | custom-call | tf_op jit(solution)/shard_map/pallas_call | solution.py:684
  47.3 1.0 %shard_map.95 = (bf16[1,128,1024]{2,1,0:T(8,128)(2,1)}, bf16[1,128,1024]{2,1,0:T(8,128)(2,1)}, f32[128,1024]{1,0:T(8,128)}) custom-call(bf16[1,128,1024]{2,1,0:T(8,128)(2,1)S(1)} %get-tuple-element.6.refs_0_, bf16[1,128,1024]{2,1,0:T(8,128)(2,1)S(1)} %get-tuple-element.7.refs_1_, f32[128,1024]{1,0:T(8,128)S(1)} %get-tuple-element.8.refs_2_), custom_call_target="tpu_custom_call" | custom-call | tf_op jit(solution)/shard_map/pallas_call | solution.py:723

commit v3 on v2

--- a/solution.py
+++ b/solution.py
@@ -267,12 +267,15 @@
     gs,
     ctx,
     logsum,
-    deltas,
+    key_sum,
+    value_sum,
     dq,
     dk,
     dv,
     part,
     part_in,
+    sums,
+    sums_in,
     slices,
     send_sem,
     recv_sem,
@@ -284,6 +287,7 @@
     rows = frames_ref.shape[1]
     full = rows * count
     scale = HEAD ** (-0.5)
+    base2 = scale * math.log2(math.e)
     sibling = dp + 1 - 2 * lax.rem(dp, 2)
     across = lax.rem(dp + 2, 4)
     across_sibling = lax.rem(sibling + 2, 4)
@@ -374,12 +378,22 @@
             def _():
                 arrive(piece_of(which, slot, at), index)
 
+    def gradient_pass(inward):
+        for at in range(2):
+            for side in range(2):
+
+                @pl.when(middle & (lower == ((side == 0) == inward)))
+                def _():
+                    owner = z - (1 - 2 * side)
+                    arrive(piece_of(1, owner, at), 12 + side * 6 + at)
+                    chain(1, side, 2, at)[1].start()
+
     def chain_pass(which, hop, at):
         chain_recv(which, hop, at)
         if hop < 3:
             chain_send(which, hop + 1, at)
 
-    weights = ((wk_ref, wk), (wv_ref, wv), (wq_ref, wq), (wo_ref, wo))
+    weights = ((wo_ref, wo), (wk_ref, wk), (wv_ref, wv), (wq_ref, wq))
 
     def half(ref, which):
         size = ref.shape[0] // 2
@@ -450,9 +464,23 @@
         mine[at] = jnp.where(real, kept, 0.0).astype(jnp.bfloat16)
     cs[z] = mine[side_at]
 
+    def whole(piece):
+        for step in (0, 5, 6):
+            weight_recv(piece, step)
+
+    def project(pool, kept, first, blocks):
+        inputs = xs[pl.ds(first, blocks)].reshape(blocks * rows, 1024)
+        start = pl.multiple_of(first * rows, rows)
+        matrix = dot(inputs, pool[...].reshape(1024, 512), 1, 0).astype(jnp.bfloat16)
+        for head in range(heads):
+            kept[head, pl.ds(start, blocks * rows), :] = matrix[:, head * HEAD : (head + 1) * HEAD]
+
+    three = jnp.where(lower, 0, 1)
+    last = jnp.where(lower, 3, 0)
+
     from_y(0)
+    chain_pass(0, 1, 0)
     from_y(1)
-    chain_pass(0, 1, 0)
     from_y(2)
     from_x(0)
     from_y(3)
@@ -473,64 +501,75 @@
     from_x(4)
     from_y(7)
     chain_pass(0, 2, 1)
-    from_x(5)
-    for piece in range(3):
-        for step in (0, 5, 6):
-            weight_recv(piece, step)
-
-    def project(first, blocks):
-        inputs = xs[pl.ds(first, blocks)].reshape(blocks * rows, 1024)
-        start = pl.multiple_of(first * rows, rows)
-        for pool, kept in ((wk, ks), (wv, vs), (wq, qs)):
-            matrix = dot(inputs, pool[...].reshape(1024, 512), 1, 0).astype(jnp.bfloat16)
-            for head in range(heads):
-                kept[head, pl.ds(start, blocks * rows), :] = matrix[
-                    :, head * HEAD : (head + 1) * HEAD
-                ]
-
-    project(jnp.where(lower, 0, 1), 3)
-    from_x(6)
-    from_x(7)
-    for step in (0, 5, 6):
-        weight_recv(3, step)
+    whole(0)
     masked = jnp.concatenate([mine[0], mine[1]], axis=1)
     matrix = dot(masked, wo[...].reshape(512, 1024), 1, 1).astype(jnp.bfloat16)
     for head in range(heads):
         gs[z, head] = matrix[:, head * HEAD : (head + 1) * HEAD]
     for at in range(2):
         chain_send(1, 1, at)
-    for at in range(2):
-        chain_pass(0, 3, at)
-    project(jnp.where(lower, 3, 0), 1)
+    from_x(5)
+    whole(1)
+    project(wk, ks, three, 3)
+    from_x(6)
+    whole(2)
+    project(wv, vs, three, 3)
+
+    def project_last():
+        project(wk, ks, last, 1)
+        project(wv, vs, last, 1)
+
+    @pl.when(middle)
+    def _():
+        project_last()
+
+    from_x(7)
+
+    @pl.when(jnp.logical_not(middle))
+    def _():
+        for at in range(2):
+            chain_pass(0, 3, at)
+        project_last()
+
+    gradient_pass(True)
+    whole(3)
+    project(wq, qs, 0, 4)
 
     def key_mask(amount):
         return lax.broadcasted_iota(jnp.int32, (amount, full), 1) < length
 
-    def part_copy(order, head, turned):
-        to_rep = other_rep if turned else rep
-        index = order * 2 + turned
-        return remote(
-            part.at[head, to_rep], part_in.at[index], 56 + index, 56 + index, (to_rep, head, z)
-        )
-
-    def forward(order, carry):
-        head = lax.rem(dp + lax.rem(order, 2) * (sibling - dp) + 2 * (1 - order // 2) + 4, 4)
+    def sibling_copy(batch):
+        sent = 56 + batch
+        return remote(part.at[batch], part_in.at[batch], sent, sent, (rep, sibling, z))
+
+    def sum_copy(which):
+        to_rep, to_dp = ((rep, across), (other_rep, across), (other_rep, dp))[which]
+        source = sums.at[which // 2, to_rep]
+        sent = 58 + which
+        return remote(source, sums_in.at[which], sent, sent, (to_rep, to_dp, z))
+
+    def attend(head):
         amount = full // 2
         usable = key_mask(amount)
         for at in range(2):
             start = at * amount
-            scores = dot(qs[head, pl.ds(start, amount), :], ks[head], 1, 1) * scale
+            scores = dot(qs[head, pl.ds(start, amount), :], ks[head], 1, 1)
             scores = jnp.where(usable, scores, MASKED_SCORE)
             maxima = jnp.max(scores, axis=1, keepdims=True)
-            exponent = jnp.exp(scores - maxima)
+            exponent = jnp.exp2((scores - maxima) * base2)
             totals = jnp.sum(exponent, axis=1, keepdims=True)
             mixed = dot(exponent.astype(jnp.bfloat16), vs[head], 1, 0)
             ctx[head, pl.ds(start, amount), :] = (mixed * (1.0 / totals)).astype(jnp.bfloat16)
-            logsum[head, pl.ds(start, amount), :] = maxima + jnp.log(totals)
+            logsum[head, pl.ds(start, amount), :] = maxima * base2 + jnp.log2(totals)
+
+    def forward(batch, carry):
+        shift = 2 * (1 - batch)
+        head = lax.rem(sibling + shift, 4)
+        attend(head)
 
         @pl.when(middle)
         def _():
-            @pl.when(order == 0)
+            @pl.when(batch == 0)
             def _():
                 for source in range(count):
 
@@ -539,28 +578,77 @@
                         arrive(cs.at[source], 52 + source)
 
             product = dot(ctx[head], cs[...].reshape(full, width), 0, 0)
+            part[batch] = product.astype(jnp.bfloat16)
+            sibling_copy(batch).start()
+
+            @pl.when(batch == 1)
+            def _():
+                gradient_pass(False)
+
+        head = lax.rem(dp + shift, 4)
+        attend(head)
+
+        @pl.when(middle)
+        def _():
+            product = dot(ctx[head], cs[...].reshape(full, width), 0, 0)
+            arrive(part_in.at[batch], 56 + batch)
+            product = product + part_in[batch].astype(jnp.float32)
             for at in range(2):
-                part[head, at] = product[:, at * 256 : (at + 1) * 256].astype(jnp.bfloat16)
-
-            @pl.when(order != 2)
+                sums[batch, at] = product[:, at * 256 : (at + 1) * 256].astype(jnp.bfloat16)
+
+            @pl.when(batch == 0)
             def _():
-                part_copy(order, head, 0).start()
-
-            part_copy(order, head, 1).start()
+                sum_copy(0).start()
+                sum_copy(1).start()
+
+            @pl.when(batch == 1)
+            def _():
+                sum_copy(2).start()
 
         return carry
 
-    lax.fori_loop(0, heads, forward, 0)
+    lax.fori_loop(0, 2, forward, 0)
+
+    @pl.when(jnp.logical_not(middle))
+    def _():
+        for at in range(2):
+            chain_recv(1, 1, at)
 
     for at in range(2):
-        chain_pass(1, 1, at)
+        chain_pass(1, 2, at)
     own = pl.ds(pl.multiple_of(z * rows, rows), rows)
     own_context = jnp.concatenate([ctx[head, own, :] for head in range(heads)], axis=1)
     attended = dot(own_context, wo[...].reshape(512, 1024), 1, 0)
     row_at = z * rows + lax.broadcasted_iota(jnp.int32, attended.shape, 0)
     attended_ref[0] = jnp.where(row_at < length, attended, 0.0).astype(jnp.bfloat16)
-    for at in range(2):
-        chain_pass(1, 2, at)
+    def row_deltas(grads, context):
+        terms = grads.astype(jnp.float32) * context.astype(jnp.float32)
+        return jnp.sum(terms, axis=1, keepdims=True)
+
+    def own_queries(head, carry):
+        grads = gs[z, head]
+        scores = dot(qs[head, own, :], ks[head], 1, 1) * base2
+        attention = jnp.where(key_mask(rows), jnp.exp2(scores - logsum[head, own, :]), 0.0)
+        grad_prob = dot(grads, vs[head], 1, 1)
+        minus = row_deltas(grads, ctx[head, own, :])
+        grad_score = (attention * (grad_prob - minus)).astype(jnp.bfloat16)
+        dq[head] = (dot(grad_score, ks[head], 1, 0) * scale).astype(jnp.bfloat16)
+        return carry
+
+    def own_keys(first, blocks, head):
+        some = pl.ds(pl.multiple_of(first * rows, rows), blocks * rows)
+        queries = qs[head, some, :]
+        grads = gs[pl.ds(first, blocks), head].reshape(blocks * rows, HEAD)
+        scores = dot(queries, ks[head, own, :], 1, 1) * base2
+        at = z * rows + lax.broadcasted_iota(jnp.int32, scores.shape, 1)
+        attention = jnp.where(at < length, jnp.exp2(scores - logsum[head, some, :]), 0.0)
+        values = dot(attention.astype(jnp.bfloat16), grads, 0, 0)
+        grad_prob = dot(grads, vs[head, own, :], 1, 1)
+        minus = row_deltas(grads, ctx[head, some, :])
+        grad_score = (attention * (grad_prob - minus)).astype(jnp.bfloat16)
+        return dot(grad_score, queries, 0, 0), values
+
+    lax.fori_loop(0, heads, own_queries, 0)
 
     mine_slice = side_at * 2 + rep
 
@@ -577,41 +665,31 @@
 
     @pl.when(middle)
     def _():
-        total = part[dp, rep].astype(jnp.float32)
-        for index in range(8):
-            if index != 4:
-                arrive(part_in.at[index], 56 + index)
-                total = total + part_in[index].astype(jnp.float32)
+        total = sums[1, rep].astype(jnp.float32)
+        for which in range(3):
+            arrive(sums_in.at[which], 58 + which)
+            total = total + sums_in[which].astype(jnp.float32)
         slices[mine_slice] = total.astype(jnp.bfloat16)
         for step in (1, 3, 2, 0):
             for turned in range(2):
                 if step + turned > 0:
                     slice_copy(step, turned).start()
 
+    def three_keys(head, carry):
+        key_sum[head], value_sum[head] = own_keys(three, 3, head)
+        return carry
+
+    lax.fori_loop(0, heads, three_keys, 0)
     for at in range(2):
         chain_pass(1, 3, at)
 
-    def backward(head, carry):
-        queries, keys, values = qs[head], ks[head], vs[head]
-        grads = gs[:, head].reshape(full, HEAD)
-        terms = grads.astype(jnp.float32) * ctx[head].astype(jnp.float32)
-        deltas[...] = jnp.sum(terms, axis=1, keepdims=True)
-        own_keys, own_values = ks[head, own, :], vs[head, own, :]
-        scores = dot(queries, own_keys, 1, 1) * scale
-        at = z * rows + lax.broadcasted_iota(jnp.int32, scores.shape, 1)
-        attention = jnp.where(at < length, jnp.exp(scores - logsum[head]), 0.0)
-        dv[head] = dot(attention.astype(jnp.bfloat16), grads, 0, 0).astype(jnp.bfloat16)
-        grad_prob = dot(grads, own_values, 1, 1)
-        grad_score = (attention * (grad_prob - deltas[...])).astype(jnp.bfloat16)
-        dk[head] = (dot(grad_score, queries, 0, 0) * scale).astype(jnp.bfloat16)
-        scores = dot(qs[head, own, :], keys, 1, 1) * scale
-        attention = jnp.where(key_mask(rows), jnp.exp(scores - logsum[head, own, :]), 0.0)
-        grad_prob = dot(gs[z, head], values, 1, 1)
-        grad_score = (attention * (grad_prob - deltas[own, :])).astype(jnp.bfloat16)
-        dq[head] = (dot(grad_score, keys, 1, 0) * scale).astype(jnp.bfloat16)
+    def last_keys(head, carry):
+        keys, values = own_keys(last, 1, head)
+        dk[head] = ((key_sum[head] + keys) * scale).astype(jnp.bfloat16)
+        dv[head] = (value_sum[head] + values).astype(jnp.bfloat16)
         return carry
 
-    lax.fori_loop(0, heads, backward, 0)
+    lax.fori_loop(0, heads, last_keys, 0)
 
     grads = [
         jnp.concatenate([kept[head] for head in range(heads)], axis=1) for kept in (dq, dk, dv)
@@ -645,9 +723,10 @@
 
     @pl.when(middle)
     def _():
-        for index in range(8):
-            if index != 4:
-                part_copy(index // 2, dp, index % 2).wait_send()
+        for batch in range(2):
+            sibling_copy(batch).wait_send()
+        for which in range(3):
+            sum_copy(which).wait_send()
 
     for at in range(count):
 
@@ -705,12 +784,15 @@
             pltpu.VMEM((4, 4, 128, HEAD), bf16),
             per_head,
             pltpu.VMEM((4, 512, 1), f32),
-            pltpu.VMEM((512, 1), f32),
+            pltpu.VMEM((4, 128, HEAD), f32),
+            pltpu.VMEM((4, 128, HEAD), f32),
             own_head,
             own_head,
             own_head,
-            pltpu.VMEM((4, 2, 128, 256), bf16),
-            pltpu.VMEM((8, 128, 256), bf16),
+            pltpu.VMEM((2, 128, 512), bf16),
+            pltpu.VMEM((2, 128, 512), bf16),
+            pltpu.VMEM((2, 2, 128, 256), bf16),
+            pltpu.VMEM((3, 128, 256), bf16),
             pltpu.VMEM((4, 128, 256), bf16),
             pltpu.SemaphoreType.DMA((72,)),
             pltpu.SemaphoreType.DMA((72,)),

time: 48.5 us -> 47.2 us (0.973)
  Pallas kernels: 47 us -> 45.8 us
    pallas_call x1, Pallas kernels: 46 us -> 44.8 us  [fused(): pl.pallas_call(fused_kernel, out_shape=(pltpu.VMEM(frames.shape, bf16), p...]
where the time goes in v3:
time: 47.2 us; the launch traced here: 47.1 us
  Pallas kernels  45.8 us (97%)
  between operations  1.29 us (3%)
    pallas_call x1, Pallas kernels, fused(): pl.pallas_call(fused_kernel, out_shape=(pltpu.VMEM(frames.shape, bf16), p...  44.8 us
    pallas_call x1, Pallas kernels, fused(): pl.pallas_call(write_kernel, out_shape=tuple((jax.ShapeDtypeStruct(r.shap...  0.99 us

profile of v3, /device:TPU:0, one launch (start us, length us, event | category | flops | bytes accessed | tf_op | source)
XLA Modules:
  0.0 47.1 jit_solution(1286250383524831674)
XLA Ops:
  1.3 44.8 %shard_map.94 = (bf16[1,128,1024]{2,1,0:T(8,128)(2,1)S(1)}, bf16[1,128,1024]{2,1,0:T(8,128)(2,1)S(1)}, f32[128,1024]{1,0:T(8,128)S(1)}) custom-call(bf16[1,128,1024]{2,1,0:T(8,128)(2,1)} %frames_ref.1, s32[1]{0:T(128)S(6)} %copy.10.length_ref, bf16[1,128,1024]{2,1,0:T(8,128)(2,1)} %cot_ref.1, bf16[256,512]{1,0:T(8,128)(2,1)} %wq_ref.1, ...), custom_call_target="tpu_custom_call" | custom-call | tf_op jit(solution)/shard_map/pallas_call | solution.py:763
  46.1 1.0 %shard_map.95 = (bf16[1,128,1024]{2,1,0:T(8,128)(2,1)}, bf16[1,128,1024]{2,1,0:T(8,128)(2,1)}, f32[128,1024]{1,0:T(8,128)}) custom-call(bf16[1,128,1024]{2,1,0:T(8,128)(2,1)S(1)} %get-tuple-element.6.refs_0_, bf16[1,128,1024]{2,1,0:T(8,128)(2,1)S(1)} %get-tuple-element.7.refs_1_, f32[128,1024]{1,0:T(8,128)S(1)} %get-tuple-element.8.refs_2_), custom_call_target="tpu_custom_call" | custom-call | tf_op jit(solution)/shard_map/pallas_call | solution.py:805

commit v4 on v3

--- a/solution.py
+++ b/solution.py
@@ -267,6 +267,9 @@
     gs,
     ctx,
     logsum,
+    exps,
+    inverse,
+    from_queries,
     key_sum,
     value_sum,
     dq,
@@ -393,7 +396,7 @@
         if hop < 3:
             chain_send(which, hop + 1, at)
 
-    weights = ((wo_ref, wo), (wk_ref, wk), (wv_ref, wv), (wq_ref, wq))
+    weights = ((wo_ref, wo), (wk_ref, wk), (wq_ref, wq), (wv_ref, wv))
 
     def half(ref, which):
         size = ref.shape[0] // 2
@@ -478,6 +481,11 @@
     three = jnp.where(lower, 0, 1)
     last = jnp.where(lower, 3, 0)
 
+    @pl.when(jnp.logical_not(middle))
+    def _():
+        cot_copy(True).start()
+        cot_copy(False).start()
+
     from_y(0)
     chain_pass(0, 1, 0)
     from_y(1)
@@ -486,11 +494,10 @@
     from_y(3)
     chain_pass(0, 1, 1)
 
-    @pl.when(jnp.logical_not(middle))
+    @pl.when(middle)
     def _():
-        cot_copy(True).start()
-
-    cot_copy(False).start()
+        cot_copy(False).start()
+
     from_x(1)
     from_y(4)
     from_x(2)
@@ -513,30 +520,48 @@
     project(wk, ks, three, 3)
     from_x(6)
     whole(2)
-    project(wv, vs, three, 3)
+    project(wq, qs, three, 3)
 
     def project_last():
         project(wk, ks, last, 1)
-        project(wv, vs, last, 1)
+        project(wq, qs, last, 1)
+
+    def key_mask(amount):
+        return lax.broadcasted_iota(jnp.int32, (amount, full), 1) < length
+
+    def exponents(head, carry):
+        amount = full // 2
+        usable = key_mask(amount)
+        for at in range(2):
+            some = pl.ds(at * amount, amount)
+            scores = dot(qs[head, some, :], ks[head], 1, 1)
+            scores = jnp.where(usable, scores, MASKED_SCORE)
+            maxima = jnp.max(scores, axis=1, keepdims=True)
+            exponent = jnp.exp2((scores - maxima) * base2)
+            totals = jnp.sum(exponent, axis=1, keepdims=True)
+            exps[head, some, :] = exponent.astype(jnp.bfloat16)
+            inverse[head, some, :] = 1.0 / totals
+            logsum[head, some, :] = maxima * base2 + jnp.log2(totals)
+        return carry
 
     @pl.when(middle)
     def _():
         project_last()
-
-    from_x(7)
+        lax.fori_loop(0, 2, exponents, 0)
+        from_x(7)
+        gradient_pass(True)
+        lax.fori_loop(2, 4, exponents, 0)
 
     @pl.when(jnp.logical_not(middle))
     def _():
+        from_x(7)
         for at in range(2):
             chain_pass(0, 3, at)
         project_last()
-
-    gradient_pass(True)
+        lax.fori_loop(0, 4, exponents, 0)
+
     whole(3)
-    project(wq, qs, 0, 4)
-
-    def key_mask(amount):
-        return lax.broadcasted_iota(jnp.int32, (amount, full), 1) < length
+    project(wv, vs, 0, 4)
 
     def sibling_copy(batch):
         sent = 56 + batch
@@ -549,22 +574,11 @@
         return remote(source, sums_in.at[which], sent, sent, (to_rep, to_dp, z))
 
     def attend(head):
-        amount = full // 2
-        usable = key_mask(amount)
-        for at in range(2):
-            start = at * amount
-            scores = dot(qs[head, pl.ds(start, amount), :], ks[head], 1, 1)
-            scores = jnp.where(usable, scores, MASKED_SCORE)
-            maxima = jnp.max(scores, axis=1, keepdims=True)
-            exponent = jnp.exp2((scores - maxima) * base2)
-            totals = jnp.sum(exponent, axis=1, keepdims=True)
-            mixed = dot(exponent.astype(jnp.bfloat16), vs[head], 1, 0)
-            ctx[head, pl.ds(start, amount), :] = (mixed * (1.0 / totals)).astype(jnp.bfloat16)
-            logsum[head, pl.ds(start, amount), :] = maxima * base2 + jnp.log2(totals)
-
-    def forward(batch, carry):
-        shift = 2 * (1 - batch)
-        head = lax.rem(sibling + shift, 4)
+        mixed = dot(exps[head], vs[head], 1, 0)
+        ctx[head] = (mixed * inverse[head]).astype(jnp.bfloat16)
+
+    def for_sibling(batch, carry):
+        head = lax.rem(sibling + 2 * (1 - batch), 4)
         attend(head)
 
         @pl.when(middle)
@@ -581,11 +595,10 @@
             part[batch] = product.astype(jnp.bfloat16)
             sibling_copy(batch).start()
 
-            @pl.when(batch == 1)
-            def _():
-                gradient_pass(False)
-
-        head = lax.rem(dp + shift, 4)
+        return carry
+
+    def for_plane(batch, carry):
+        head = lax.rem(dp + 2 * (1 - batch), 4)
         attend(head)
 
         @pl.when(middle)
@@ -607,7 +620,9 @@
 
         return carry
 
-    lax.fori_loop(0, 2, forward, 0)
+    lax.fori_loop(0, 2, for_sibling, 0)
+    gradient_pass(False)
+    lax.fori_loop(0, 2, for_plane, 0)
 
     @pl.when(jnp.logical_not(middle))
     def _():
@@ -670,16 +685,21 @@
             arrive(sums_in.at[which], 58 + which)
             total = total + sums_in[which].astype(jnp.float32)
         slices[mine_slice] = total.astype(jnp.bfloat16)
-        for step in (1, 3, 2, 0):
-            for turned in range(2):
-                if step + turned > 0:
-                    slice_copy(step, turned).start()
+        low, high, mate = lax.rem(count - z, count), 3 - z, jnp.where(lower, 1, 3)
+        for step in (low, mate, high):
+            for turned in (1, 0):
+                slice_copy(step, turned).start()
+        slice_copy(0, 1).start()
 
     def three_keys(head, carry):
         key_sum[head], value_sum[head] = own_keys(three, 3, head)
         return carry
 
     lax.fori_loop(0, heads, three_keys, 0)
+    by_query = jnp.concatenate([dq[head] for head in range(heads)], axis=1)
+    for shard in range(4):
+        from_queries[:, shard * 256 : (shard + 1) * 256] = dot(by_query, wq[shard], 1, 1)
+
     for at in range(2):
         chain_pass(1, 3, at)
 
@@ -691,16 +711,14 @@
 
     lax.fori_loop(0, heads, last_keys, 0)
 
-    grads = [
-        jnp.concatenate([kept[head] for head in range(heads)], axis=1) for kept in (dq, dk, dv)
-    ]
+    by_key, by_value = (
+        jnp.concatenate([kept[head] for head in range(heads)], axis=1) for kept in (dk, dv)
+    )
     for shard in range(4):
-        added = (
-            dot(grads[0], wq[shard], 1, 1)
-            + dot(grads[1], wk[shard], 1, 1)
-            + dot(grads[2], wv[shard], 1, 1)
-        )
-        grad_frames_ref[0, :, shard * 256 : (shard + 1) * 256] = added.astype(jnp.bfloat16)
+        columns = slice(shard * 256, (shard + 1) * 256)
+        added = dot(by_key, wk[shard], 1, 1) + dot(by_value, wv[shard], 1, 1)
+        added = added + from_queries[:, columns]
+        grad_frames_ref[0, :, columns] = added.astype(jnp.bfloat16)
 
     for piece in range(4):
         for step in range(7):
@@ -784,6 +802,9 @@
             pltpu.VMEM((4, 4, 128, HEAD), bf16),
             per_head,
             pltpu.VMEM((4, 512, 1), f32),
+            pltpu.VMEM((4, 512, 512), bf16),
+            pltpu.VMEM((4, 512, 1), f32),
+            pltpu.VMEM((128, 1024), f32),
             pltpu.VMEM((4, 128, HEAD), f32),
             pltpu.VMEM((4, 128, HEAD), f32),
             own_head,

time: 47.2 us -> 46.1 us (0.977)
  Pallas kernels: 45.8 us -> 44.7 us
    pallas_call x1, Pallas kernels: 44.8 us -> 43.7 us  [fused(): pl.pallas_call(fused_kernel, out_shape=(pltpu.VMEM(frames.shape, bf16), p...]
where the time goes in v4:
time: 46.1 us; the launch traced here: 46 us
  Pallas kernels  44.7 us (97%)
  between operations  1.29 us (3%)
    pallas_call x1, Pallas kernels, fused(): pl.pallas_call(fused_kernel, out_shape=(pltpu.VMEM(frames.shape, bf16), p...  43.7 us
    pallas_call x1, Pallas kernels, fused(): pl.pallas_call(write_kernel, out_shape=tuple((jax.ShapeDtypeStruct(r.shap...  0.99 us

profile of v4, /device:TPU:0, one launch (start us, length us, event | category | flops | bytes accessed | tf_op | source)
XLA Modules:
  0.0 46.0 jit_solution(14054937973569043427)
XLA Ops:
  1.3 43.7 %shard_map.94 = (bf16[1,128,1024]{2,1,0:T(8,128)(2,1)S(1)}, bf16[1,128,1024]{2,1,0:T(8,128)(2,1)S(1)}, f32[128,1024]{1,0:T(8,128)S(1)}) custom-call(bf16[1,128,1024]{2,1,0:T(8,128)(2,1)} %frames_ref.1, s32[1]{0:T(128)S(6)} %copy.10.length_ref, bf16[1,128,1024]{2,1,0:T(8,128)(2,1)} %cot_ref.1, bf16[256,512]{1,0:T(8,128)(2,1)} %wq_ref.1, ...), custom_call_target="tpu_custom_call" | custom-call | tf_op jit(solution)/shard_map/pallas_call | solution.py:781
  45.0 1.0 %shard_map.95 = (bf16[1,128,1024]{2,1,0:T(8,128)(2,1)}, bf16[1,128,1024]{2,1,0:T(8,128)(2,1)}, f32[128,1024]{1,0:T(8,128)}) custom-call(bf16[1,128,1024]{2,1,0:T(8,128)(2,1)S(1)} %get-tuple-element.6.refs_0_, bf16[1,128,1024]{2,1,0:T(8,128)(2,1)S(1)} %get-tuple-element.7.refs_1_, f32[128,1024]{1,0:T(8,128)S(1)} %get-tuple-element.8.refs_2_), custom_call_target="tpu_custom_call" | custom-call | tf_op jit(solution)/shard_map/pallas_call | solution.py:826

commit v5 on v4

--- a/solution.py
+++ b/solution.py
@@ -490,9 +490,9 @@
     chain_pass(0, 1, 0)
     from_y(1)
     from_y(2)
+    chain_pass(0, 1, 1)
     from_x(0)
     from_y(3)
-    chain_pass(0, 1, 1)
 
     @pl.when(middle)
     def _():
@@ -502,12 +502,11 @@
     from_y(4)
     from_x(2)
     from_y(5)
-    chain_pass(0, 2, 0)
     from_x(3)
     from_y(6)
+    chain_pass(0, 2, 0)
     from_x(4)
     from_y(7)
-    chain_pass(0, 2, 1)
     whole(0)
     masked = jnp.concatenate([mine[0], mine[1]], axis=1)
     matrix = dot(masked, wo[...].reshape(512, 1024), 1, 1).astype(jnp.bfloat16)
@@ -516,9 +515,10 @@
     for at in range(2):
         chain_send(1, 1, at)
     from_x(5)
+    chain_pass(0, 2, 1)
     whole(1)
+    from_x(6)
     project(wk, ks, three, 3)
-    from_x(6)
     whole(2)
     project(wq, qs, three, 3)
 
@@ -577,52 +577,46 @@
         mixed = dot(exps[head], vs[head], 1, 0)
         ctx[head] = (mixed * inverse[head]).astype(jnp.bfloat16)
 
-    def for_sibling(batch, carry):
-        head = lax.rem(sibling + 2 * (1 - batch), 4)
-        attend(head)
-
-        @pl.when(middle)
-        def _():
-            @pl.when(batch == 0)
+    def pair_product(first):
+        far = lax.rem(first + 2, 4)
+        pair = jnp.concatenate([ctx[far], ctx[first]], axis=1)
+        return dot(pair, cs[...].reshape(full, width), 0, 0)
+
+    attend(lax.rem(sibling + 2, 4))
+    attend(sibling)
+
+    @pl.when(middle)
+    def _():
+        for source in range(count):
+
+            @pl.when(z != source)
             def _():
-                for source in range(count):
-
-                    @pl.when(z != source)
-                    def _():
-                        arrive(cs.at[source], 52 + source)
-
-            product = dot(ctx[head], cs[...].reshape(full, width), 0, 0)
-            part[batch] = product.astype(jnp.bfloat16)
+                arrive(cs.at[source], 52 + source)
+
+        product = pair_product(sibling)
+        for batch in range(2):
+            part[batch] = product[batch * 128 : (batch + 1) * 128].astype(jnp.bfloat16)
             sibling_copy(batch).start()
 
-        return carry
-
-    def for_plane(batch, carry):
-        head = lax.rem(dp + 2 * (1 - batch), 4)
-        attend(head)
-
-        @pl.when(middle)
-        def _():
-            product = dot(ctx[head], cs[...].reshape(full, width), 0, 0)
+    gradient_pass(False)
+    attend(lax.rem(dp + 2, 4))
+    attend(dp)
+
+    @pl.when(middle)
+    def _():
+        product = pair_product(dp)
+        for batch in range(2):
             arrive(part_in.at[batch], 56 + batch)
-            product = product + part_in[batch].astype(jnp.float32)
+            kept = product[batch * 128 : (batch + 1) * 128]
+            kept = kept + part_in[batch].astype(jnp.float32)
             for at in range(2):
-                sums[batch, at] = product[:, at * 256 : (at + 1) * 256].astype(jnp.bfloat16)
-
-            @pl.when(batch == 0)
-            def _():
+                sums[batch, at] = kept[:, at * 256 : (at + 1) * 256].astype(jnp.bfloat16)
+            if batch == 0:
                 sum_copy(0).start()
                 sum_copy(1).start()
-
-            @pl.when(batch == 1)
-            def _():
+            else:
                 sum_copy(2).start()
 
-        return carry
-
-    lax.fori_loop(0, 2, for_sibling, 0)
-    gradient_pass(False)
-    lax.fori_loop(0, 2, for_plane, 0)
 
     @pl.when(jnp.logical_not(middle))
     def _():

time: 46.1 us -> 44.9 us (0.974)
  Pallas kernels: 44.7 us -> 43.5 us
    pallas_call x1, Pallas kernels: 43.7 us -> 42.5 us  [fused(): pl.pallas_call(fused_kernel, out_shape=(pltpu.VMEM(frames.shape, bf16), p...]
where the time goes in v5:
time: 44.9 us; the launch traced here: 44.8 us
  Pallas kernels  43.5 us (97%)
  between operations  1.29 us (3%)
    pallas_call x1, Pallas kernels, fused(): pl.pallas_call(fused_kernel, out_shape=(pltpu.VMEM(frames.shape, bf16), p...  42.5 us
    pallas_call x1, Pallas kernels, fused(): pl.pallas_call(write_kernel, out_shape=tuple((jax.ShapeDtypeStruct(r.shap...  0.99 us

profile of v5, /device:TPU:0, one launch (start us, length us, event | category | flops | bytes accessed | tf_op | source)
XLA Modules:
  0.0 44.8 jit_solution(4343161210915536547)
XLA Ops:
  1.3 42.5 %shard_map.94 = (bf16[1,128,1024]{2,1,0:T(8,128)(2,1)S(1)}, bf16[1,128,1024]{2,1,0:T(8,128)(2,1)S(1)}, f32[128,1024]{1,0:T(8,128)S(1)}) custom-call(bf16[1,128,1024]{2,1,0:T(8,128)(2,1)} %frames_ref.1, s32[1]{0:T(128)S(6)} %copy.10.length_ref, bf16[1,128,1024]{2,1,0:T(8,128)(2,1)} %cot_ref.1, bf16[256,512]{1,0:T(8,128)(2,1)} %wq_ref.1, ...), custom_call_target="tpu_custom_call" | custom-call | tf_op jit(solution)/shard_map/pallas_call | solution.py:775
  43.8 1.0 %shard_map.95 = (bf16[1,128,1024]{2,1,0:T(8,128)(2,1)}, bf16[1,128,1024]{2,1,0:T(8,128)(2,1)}, f32[128,1024]{1,0:T(8,128)}) custom-call(bf16[1,128,1024]{2,1,0:T(8,128)(2,1)S(1)} %get-tuple-element.6.refs_0_, bf16[1,128,1024]{2,1,0:T(8,128)(2,1)S(1)} %get-tuple-element.7.refs_1_, f32[128,1024]{1,0:T(8,128)S(1)} %get-tuple-element.8.refs_2_), custom_call_target="tpu_custom_call" | custom-call | tf_op jit(solution)/shard_map/pallas_call | solution.py:820

commit v6 on v5

--- a/solution.py
+++ b/solution.py
@@ -547,10 +547,11 @@
     @pl.when(middle)
     def _():
         project_last()
-        lax.fori_loop(0, 2, exponents, 0)
-        from_x(7)
-        gradient_pass(True)
-        lax.fori_loop(2, 4, exponents, 0)
+        for head in range(4):
+            exponents(head, 0)
+            if head == 1:
+                from_x(7)
+                gradient_pass(True)
 
     @pl.when(jnp.logical_not(middle))
     def _():
@@ -558,7 +559,8 @@
         for at in range(2):
             chain_pass(0, 3, at)
         project_last()
-        lax.fori_loop(0, 4, exponents, 0)
+        for head in range(4):
+            exponents(head, 0)
 
     whole(3)
     project(wv, vs, 0, 4)

time: 44.9 us -> 44.3 us (0.987)
  Pallas kernels: 43.5 us -> 42.8 us
    pallas_call x1, Pallas kernels: 42.5 us -> 41.9 us  [fused(): pl.pallas_call(fused_kernel, out_shape=(pltpu.VMEM(frames.shape, bf16), p...]
where the time goes in v6:
time: 44.3 us; the launch traced here: 44.1 us
  Pallas kernels  42.8 us (97%)
  between operations  1.29 us (3%)
    pallas_call x1, Pallas kernels, fused(): pl.pallas_call(fused_kernel, out_shape=(pltpu.VMEM(frames.shape, bf16), p...  41.9 us
    pallas_call x1, Pallas kernels, fused(): pl.pallas_call(write_kernel, out_shape=tuple((jax.ShapeDtypeStruct(r.shap...  0.99 us

profile of v6, /device:TPU:0, one launch (start us, length us, event | category | flops | bytes accessed | tf_op | source)
XLA Modules:
  0.0 44.1 jit_solution(7360848281405041608)
XLA Ops:
  1.3 41.9 %shard_map.94 = (bf16[1,128,1024]{2,1,0:T(8,128)(2,1)S(1)}, bf16[1,128,1024]{2,1,0:T(8,128)(2,1)S(1)}, f32[128,1024]{1,0:T(8,128)S(1)}) custom-call(bf16[1,128,1024]{2,1,0:T(8,128)(2,1)} %frames_ref.1, s32[1]{0:T(128)S(6)} %copy.10.length_ref, bf16[1,128,1024]{2,1,0:T(8,128)(2,1)} %cot_ref.1, bf16[256,512]{1,0:T(8,128)(2,1)} %wq_ref.1, ...), custom_call_target="tpu_custom_call" | custom-call | tf_op jit(solution)/shard_map/pallas_call | solution.py:777
  43.1 1.0 %shard_map.95 = (bf16[1,128,1024]{2,1,0:T(8,128)(2,1)}, bf16[1,128,1024]{2,1,0:T(8,128)(2,1)}, f32[128,1024]{1,0:T(8,128)}) custom-call(bf16[1,128,1024]{2,1,0:T(8,128)(2,1)S(1)} %get-tuple-element.6.refs_0_, bf16[1,128,1024]{2,1,0:T(8,128)(2,1)S(1)} %get-tuple-element.7.refs_1_, f32[128,1024]{1,0:T(8,128)S(1)} %get-tuple-element.8.refs_2_), custom_call_target="tpu_custom_call" | custom-call | tf_op jit(solution)/shard_map/pallas_call | solution.py:822

commit v7 on v6

--- a/solution.py
+++ b/solution.py
@@ -551,6 +551,7 @@
             exponents(head, 0)
             if head == 1:
                 from_x(7)
+            if head == 3:
                 gradient_pass(True)
 
     @pl.when(jnp.logical_not(middle))

time: 44.3 us -> 44.3 us (level)
  no operation moved by 1% of the time
where the time goes in v7:
time: 44.3 us; the launch traced here: 44.1 us
  Pallas kernels  42.8 us (97%)
  between operations  1.29 us (3%)
    pallas_call x1, Pallas kernels, fused(): pl.pallas_call(fused_kernel, out_shape=(pltpu.VMEM(frames.shape, bf16), p...  41.9 us
    pallas_call x1, Pallas kernels, fused(): pl.pallas_call(write_kernel, out_shape=tuple((jax.ShapeDtypeStruct(r.shap...  0.99 us

profile of v7, /device:TPU:0, one launch (start us, length us, event | category | flops | bytes accessed | tf_op | source)
XLA Modules:
  0.0 44.1 jit_solution(3966914139748879300)
XLA Ops:
  1.3 41.9 %shard_map.94 = (bf16[1,128,1024]{2,1,0:T(8,128)(2,1)S(1)}, bf16[1,128,1024]{2,1,0:T(8,128)(2,1)S(1)}, f32[128,1024]{1,0:T(8,128)S(1)}) custom-call(bf16[1,128,1024]{2,1,0:T(8,128)(2,1)} %frames_ref.1, s32[1]{0:T(128)S(6)} %copy.10.length_ref, bf16[1,128,1024]{2,1,0:T(8,128)(2,1)} %cot_ref.1, bf16[256,512]{1,0:T(8,128)(2,1)} %wq_ref.1, ...), custom_call_target="tpu_custom_call" | custom-call | tf_op jit(solution)/shard_map/pallas_call | solution.py:778
  43.1 1.0 %shard_map.95 = (bf16[1,128,1024]{2,1,0:T(8,128)(2,1)}, bf16[1,128,1024]{2,1,0:T(8,128)(2,1)}, f32[128,1024]{1,0:T(8,128)}) custom-call(bf16[1,128,1024]{2,1,0:T(8,128)(2,1)S(1)} %get-tuple-element.6.refs_0_, bf16[1,128,1024]{2,1,0:T(8,128)(2,1)S(1)} %get-tuple-element.7.refs_1_, f32[128,1024]{1,0:T(8,128)S(1)} %get-tuple-element.8.refs_2_), custom_call_target="tpu_custom_call" | custom-call | tf_op jit(solution)/shard_map/pallas_call | solution.py:823
